TPU v7x, 256 devices: a whole 4x4x8 slice. The times are simulated.
256 devices in a mesh: gossip: 64 (over y_hi, z, x), fsdp: 4 (over y_lo, core).
Axes of the slice: x: 4, y: 4 (y_hi: 2, y_lo: 2; y = y_hi * 2 + y_lo), z: 8, core: 2. Of those that a mesh axis runs over, the one named last changes fastest.
Arguments:
- numerator: float32 [64, 2048, 2048], P('gossip', 'fsdp'), may hold values from -6 to 6
- push_weight: bfloat16 [64], P('gossip'), may hold values from 0.5 to 2
- hidden_in: bfloat16 [2, 64, 1024, 2048], P(None, 'gossip', 'fsdp'), may hold values from -6 to 6
- targets: bfloat16 [2, 64, 1024, 2048], P(None, 'gossip', 'fsdp'), may hold values from -6 to 6
- exponents: int32 [2], replicated, may hold values from 0 to 2
Outputs:
- params_out: float32 [64, 2048, 2048], P('gossip', 'fsdp')
- weight_out: float32 [64], P('gossip')
Inputs may be any that keep to these rules, and one draw needn't show every extreme that they name: The push of step t goes 2**exponents[t] replicas further along, wrapping around.
All inputs are finite; a program needn't handle non-finite values.
Results may differ from a plain program's by a relative error of at most 0.014.
Values may be sent and summed in bfloat16 or wider, within the bound.
No kernel may reach another device: no remote copies, remote signals or barrier semaphores. Data moves between devices by JAX's collectives and lax.ppermute only.
A program may use at most 128 MiB of HBM per device.

v0:
```python
from functools import partial
import math

import jax
import jax.numpy as jnp
from jax import lax
from jax.sharding import PartitionSpec as P

STEPS = 2
EXPONENTS = 3


learning_rate = 0.5
epsilon = 1e-06


def for_sending(x):

    def short(part):
        return part.astype(jnp.bfloat16) if part.dtype == jnp.float32 else part

    return jax.tree.map(short, x)


def shifted(block, axis, distance):
    devices = range(lax.axis_size(axis))
    route = [((i - distance) % len(devices), i) for i in devices]
    return lax.ppermute(block, axis, route)


def normalize(hidden):
    values = hidden.astype(jnp.float32)
    scaled = values * lax.rsqrt(jnp.mean(values * values, axis=-1, keepdims=True) + epsilon)
    return scaled.astype(jnp.bfloat16)


def residual_term(preact, goal):
    sigma = jax.nn.sigmoid(preact)
    slope = sigma * (1.0 + preact * (1.0 - sigma))
    return ((preact * sigma - goal.astype(jnp.float32)) * slope).astype(jnp.bfloat16)


def send_on(rows, weight, distance):
    return (
        shifted(for_sending(rows), "gossip", distance).astype(rows.dtype),
        shifted(for_sending(weight), "gossip", distance).astype(weight.dtype),
    )


def per_device(numerator, push_weight, hidden_in, targets, exponents):
    numerators = numerator[0]
    weight = push_weight.astype(jnp.float32)
    root_width = math.sqrt(numerators.shape[1])
    branches = [partial(send_on, distance=1 << power) for power in range(EXPONENTS)]
    pending_rows = None
    pending_weight = None
    for step in range(STEPS):
        current = (numerators / weight[0]).astype(jnp.bfloat16)
        normed = normalize(hidden_in[step, 0])
        goal_rows = targets[step, 0]
        preact = (
            lax.dot_general(
                normed,
                lax.all_gather(current, "fsdp", axis=0, tiled=True),
                (((1,), (1,)), ((), ())),
                preferred_element_type=jnp.float32,
            )
            / root_width
        )
        delta = residual_term(preact, goal_rows)
        gradient = (
            lax.psum_scatter(
                lax.dot_general(
                    delta, normed, (((0,), (0,)), ((), ())), preferred_element_type=jnp.float32
                ).astype(jnp.bfloat16),
                "fsdp",
                scatter_dimension=0,
                tiled=True,
            ).astype(jnp.float32)
            / root_width
        )
        halved = (numerators - learning_rate * gradient) * 0.5
        arrived_rows, arrived_weight = lax.switch(
            exponents[step],
            branches,
            halved.astype(jnp.bfloat16),
            (weight * 0.5).astype(jnp.bfloat16),
        )
        numerators = halved
        weight = weight * 0.5
        if step > 0:
            numerators = numerators + pending_rows.astype(jnp.float32)
            weight = weight + pending_weight.astype(jnp.float32)
        pending_rows = arrived_rows
        pending_weight = arrived_weight
    numerators = numerators + pending_rows.astype(jnp.float32)
    weight = weight + pending_weight.astype(jnp.float32)
    return ((numerators / weight[0])[None], weight)


def solution(mesh):
    in_specs = (
        P("gossip", "fsdp", None),
        P("gossip"),
        P(None, "gossip", "fsdp", None),
        P(None, "gossip", "fsdp", None),
        P(),
    )
    out_specs = (P("gossip", "fsdp", None), P("gossip"))
    return jax.shard_map(
        per_device, mesh=mesh, in_specs=in_specs, out_specs=out_specs, check_vma=False
    )
```

profile of v0, /device:TPU:1, one launch (start us, length us, event | category | flops | bytes accessed | tf_op | source)
XLA Modules:
  0.0 501.4 jit_solution(13548049981425877420)
XLA Ops:
  7.2 0.0 all-gather.3.cloned.1.call-start
  7.9 4.0 fusion.2
  11.9 0.0 copy-start.1
  11.9 0.0 all-gather.3.cloned.1.call-update
  11.9 0.0 reduce-scatter.3.cloned.1.call-start
  11.9 1.5 copy-done.1
  13.4 0.5 fusion.7
  13.9 86.3 %all-gather.3.cloned.1.call-done = bf16[2048,2048]{1,0:T(8,128)(2,1)} async-done(((bf16[512,2048]{1,0:T(8,128)(2,1)}), bf16[2048,2048]{1,0:T(8,128)(2,1)}) %all-gather.3.cloned.1.call-update) | async-done | bytes 8388624 | tf_op jit(solution)/shard_map/all_gather | solution.py:64
  100.2 10.0 %convolution_convert_fusion.1 = bf16[2048,2048]{1,0:T(8,128)(2,1)} fusion(bf16[2048,2048]{1,0:T(8,128)(2,1)} %all-gather.3.cloned.1.call-done, bf16[2,1,256,2048]{3,2,1,0:T(8,128)(2,1)} %param.14, f32[256]{0:T(256)S(1)} %add_rsqrt_fusion.1, bf16[2,1,256,2048]{3,2,1,0:T(8,128)(2,1)S(1)} %copy-done.1), kind=kOutput, calls=%fused_computation.1 | convolution fusion | flops 4309123072 | bytes 19924992 | tf_op jit(solution)/shard_map/dot_general | solution.py:73
  110.2 0.0 reduce-scatter.3.cloned.1.call-update
  110.3 0.0 all-gather.5.cloned.1.call-start
  110.3 82.5 %reduce-scatter.3.cloned.1.call-done = bf16[512,2048]{1,0:T(8,128)(2,1)} async-done(((bf16[2048,2048]{1,0:T(8,128)(2,1)}), bf16[512,2048]{1,0:T(8,128)(2,1)}) %reduce-scatter.3.cloned.1.call-update) | async-done | bytes 2097168 | tf_op jit(solution)/shard_map/reduce_scatter | solution.py:72
  192.8 5.0 %divide_convert_fusion = bf16[512,2048]{1,0:T(8,128)(2,1)} fusion(f32[]{:T(128)} %bitcast.7, bf16[512,2048]{1,0:T(8,128)(2,1)} %reduce-scatter.3.cloned.1.call-done, f32[1,512,2048]{2,1,0:T(8,128)} %param.11), kind=kLoop, calls=%fused_computation.11 | loop fusion | flops 6291456 | bytes 8388612 | tf_op jit(solution)/shard_map/convert_element_type | solution.py:58
  197.8 0.0 all-gather.5.cloned.1.call-update
  197.8 0.0 reduce-scatter.5.cloned.1.call-start
  197.9 85.2 %all-gather.5.cloned.1.call-done = bf16[2048,2048]{1,0:T(8,128)(2,1)} async-done(((bf16[512,2048]{1,0:T(8,128)(2,1)}), bf16[2048,2048]{1,0:T(8,128)(2,1)}) %all-gather.5.cloned.1.call-update) | async-done | bytes 8388624 | tf_op jit(solution)/shard_map/all_gather | solution.py:64
  283.1 10.0 %convolution_convert_fusion = bf16[2048,2048]{1,0:T(8,128)(2,1)} fusion(bf16[2048,2048]{1,0:T(8,128)(2,1)} %all-gather.5.cloned.1.call-done, bf16[2,1,256,2048]{3,2,1,0:T(8,128)(2,1)} %param.14, f32[256]{0:T(256)S(1)} %add_rsqrt_fusion, bf16[2,1,256,2048]{3,2,1,0:T(8,128)(2,1)S(1)} %copy-done.1), kind=kOutput, calls=%fused_computation | convolution fusion | flops 4309123072 | bytes 19924992 | tf_op jit(solution)/shard_map/dot_general | solution.py:73
  293.1 0.0 copy-start.2
  293.1 0.0 copy-start
  293.1 0.0 reduce-scatter.5.cloned.1.call-update
  293.2 0.6 copy-done.2
  293.8 0.6 fusion.42
  295.7 80.0 %reduce-scatter.5.cloned.1.call-done = bf16[512,2048]{1,0:T(8,128)(2,1)} async-done(((bf16[2048,2048]{1,0:T(8,128)(2,1)}), bf16[512,2048]{1,0:T(8,128)(2,1)}) %reduce-scatter.5.cloned.1.call-update) | async-done | bytes 2097168 | tf_op jit(solution)/shard_map/reduce_scatter | solution.py:72
  375.7 0.0 copy-done
  375.7 5.7 %fusion.41 = (bf16[512,2048]{1,0:T(8,128)(2,1)S(1)}, bf16[512,2048]{1,0:T(8,128)(2,1)}) fusion(bf16[512,2048]{1,0:T(8,128)(2,1)S(1)} %copy-done, f32[1,512,2048]{2,1,0:T(8,128)} %param.11, bf16[512,2048]{1,0:T(8,128)(2,1)} %reduce-scatter.5.cloned.1.call-done), kind=kLoop, calls=%fused_computation.49 | loop fusion | flops 10485760 | bytes 12582912 | tf_op jit(solution)/shard_map/convert_element_type | solution.py:86
  381.3 52.9 %conditional.8 = (bf16[512,2048]{1,0:T(8,128)(2,1)}, bf16[1]{0:T(256)(128)(2,1)}) conditional(s32[]{:T(128)} %bitcast.9, (bf16[512,2048]{1,0:T(8,128)(2,1)S(1)}, bf16[1]{0:T(256)(128)(2,1)}) %tuple.72, (bf16[512,2048]{1,0:T(8,128)(2,1)S(1)}, bf16[1]{0:T(256)(128)(2,1)}) %tuple.72, (bf16[512,2048]{1,0:T(8,128)(2,1)S(1)}, ...), branch_computations={%region_4.0_spmd, %region_5.0_spmd, %region_6.0_spmd} | conditional | bytes 8388712
  381.3 1.2 collective-permute-start
  382.5 44.7 %collective-permute-start.1 = (bf16[1]{0:T(256)(128)(2,1)}, bf16[1]{0:T(256)(128)(2,1)}, u32[]{:S(2)}, u32[]{:S(2)}) collective-permute-start(bf16[1]{0:T(256)(128)(2,1)} %get-tuple-element.49), channel_id=1, source_target_pairs={{252,0},{0,4},{4,8},{8,12},{12,16},{16,20},{20,24},{24,28},{28,32}... | collective-permute-start | bytes 14 | tf_op jit(solution)/shard_map/cond/branch_0_fun/ppermute | solution.py:28
  427.2 7.1 %collective-permute-done.1 = bf16[1]{0:T(256)(128)(2,1)} collective-permute-done((bf16[1]{0:T(256)(128)(2,1)}, bf16[1]{0:T(256)(128)(2,1)}, u32[]{:S(2)}, u32[]{:S(2)}) %collective-permute-start.1) | collective-permute-done | bytes 34 | tf_op jit(solution)/shard_map/cond/branch_0_fun/ppermute | solution.py:28
  434.3 0.0 collective-permute-done
  434.9 50.0 %conditional.9 = (bf16[512,2048]{1,0:T(8,128)(2,1)}, bf16[1]{0:T(256)(128)(2,1)}) conditional(s32[]{:T(128)} %bitcast.10, (bf16[512,2048]{1,0:T(8,128)(2,1)}, bf16[1]{0:T(256)(128)(2,1)}) %tuple.73, (bf16[512,2048]{1,0:T(8,128)(2,1)}, bf16[1]{0:T(256)(128)(2,1)}) %tuple.73, (bf16[512,2048]{1,0:T(8,128)(2,1)}, ...), branch_computations={%region_7.0_spmd, %region_8.0_spmd, %region_9.0_spmd} | conditional | bytes 8388712
  434.9 0.1 collective-permute-start.10
  435.0 44.4 %collective-permute-start.11 = (bf16[1]{0:T(256)(128)(2,1)}, bf16[1]{0:T(256)(128)(2,1)}, u32[]{:S(2)}, u32[]{:S(2)}) collective-permute-start(bf16[1]{0:T(256)(128)(2,1)} %get-tuple-element.59), channel_id=1, source_target_pairs={{240,0},{244,4},{248,8},{252,12},{0,16},{4,20},{8,24},{12,28},{16,... | collective-permute-start | bytes 14 | tf_op jit(solution)/shard_map/cond/branch_2_fun/ppermute | solution.py:28
  479.4 5.5 %collective-permute-done.11 = bf16[1]{0:T(256)(128)(2,1)} collective-permute-done((bf16[1]{0:T(256)(128)(2,1)}, bf16[1]{0:T(256)(128)(2,1)}, u32[]{:S(2)}, u32[]{:S(2)}) %collective-permute-start.11) | collective-permute-done | bytes 34 | tf_op jit(solution)/shard_map/cond/branch_2_fun/ppermute | solution.py:28
  484.9 0.0 collective-permute-done.10
  485.6 8.1 %fusion.1 = f32[1,512,2048]{2,1,0:T(8,128)} fusion(bf16[512,2048]{1,0:T(8,128)(2,1)} %get-tuple-element.80, bf16[512,2048]{1,0:T(8,128)(2,1)} %get-tuple-element.76, bf16[512,2048]{1,0:T(8,128)(2,1)} %reduce-scatter.5.cloned.1.call-done, f32[]{:T(128)} %bitcast.11, bf16[512,2048]{1,0:T(8,128)(2,1)S(1)} %copy-done, f32[1,512,2048]{2,1,0:T(8,128)} %param.11), kind=kLoop, calls=%fused_computation.4 | loop fusion | flops 13631488 | bytes 16777220 | tf_op jit(solution)/shard_map/broadcast_in_dim | solution.py:98
  (2 shorter events, 0.0 us)
Async XLA Ops:
  7.2 93.1 %all-gather.3.cloned.1.call-start = ((), (), s32[]{:S(2)}) async-start(), calls=%async_computation.2 | async-start | bytes 10485760 | tf_op jit(solution)/shard_map/all_gather | solution.py:64
  11.9 1.6 copy-start.1
  11.9 180.9 %reduce-scatter.3.cloned.1.call-start = ((), (), s32[]{:S(2)}) async-start(), calls=%async_computation.3 | async-start | bytes 10485760 | tf_op jit(solution)/shard_map/reduce_scatter | solution.py:72
  110.3 172.8 %all-gather.5.cloned.1.call-start = ((), (), s32[]{:S(2)}) async-start(), calls=%async_computation.4 | async-start | bytes 10485760 | tf_op jit(solution)/shard_map/all_gather | solution.py:64
  197.8 177.8 %reduce-scatter.5.cloned.1.call-start = ((), (), s32[]{:S(2)}) async-start(), calls=%async_computation.5 | async-start | bytes 10485760 | tf_op jit(solution)/shard_map/reduce_scatter | solution.py:72
  293.1 0.7 copy-start.2
  293.1 82.6 %copy-start = (bf16[512,2048]{1,0:T(8,128)(2,1)S(1)}, bf16[512,2048]{1,0:T(8,128)(2,1)}, u32[]{:S(2)}) copy-start(bf16[512,2048]{1,0:T(8,128)(2,1)} %reduce-scatter.3.cloned.1.call-done) | copy-start | bytes 6291460
  381.3 52.9 %collective-permute-start = (bf16[512,2048]{1,0:T(8,128)(2,1)S(1)}, bf16[512,2048]{1,0:T(8,128)(2,1)}, u32[]{:S(2)}, u32[]{:S(2)}) collective-permute-start(bf16[512,2048]{1,0:T(8,128)(2,1)S(1)} %get-tuple-element.48), channel_id=1, source_target_pairs={{252,0},{0,4},{4,8},{8,12},{12,16},{16,20},{20,24},{24,28},{28,32}... | collective-permute-start | bytes 6291464 | tf_op jit(solution)/shard_map/cond/branch_0_fun/ppermute | solution.py:28
  382.5 51.7 %collective-permute-start.1 = (bf16[1]{0:T(256)(128)(2,1)}, bf16[1]{0:T(256)(128)(2,1)}, u32[]{:S(2)}, u32[]{:S(2)}) collective-permute-start(bf16[1]{0:T(256)(128)(2,1)} %get-tuple-element.49), channel_id=1, source_target_pairs={{252,0},{0,4},{4,8},{8,12},{12,16},{16,20},{20,24},{24,28},{28,32}... | collective-permute-start | bytes 14 | tf_op jit(solution)/shard_map/cond/branch_0_fun/ppermute | solution.py:28
  434.9 50.0 %collective-permute-start.10 = (bf16[512,2048]{1,0:T(8,128)(2,1)}, bf16[512,2048]{1,0:T(8,128)(2,1)}, u32[]{:S(2)}, u32[]{:S(2)}) collective-permute-start(bf16[512,2048]{1,0:T(8,128)(2,1)} %get-tuple-element.58), channel_id=1, source_target_pairs={{240,0},{244,4},{248,8},{252,12},{0,16},{4,20},{8,24},{12,28},{16,... | collective-permute-start | bytes 6291464 | tf_op jit(solution)/shard_map/cond/branch_2_fun/ppermute | solution.py:28
  435.0 49.9 %collective-permute-start.11 = (bf16[1]{0:T(256)(128)(2,1)}, bf16[1]{0:T(256)(128)(2,1)}, u32[]{:S(2)}, u32[]{:S(2)}) collective-permute-start(bf16[1]{0:T(256)(128)(2,1)} %get-tuple-element.59), channel_id=1, source_target_pairs={{240,0},{244,4},{248,8},{252,12},{0,16},{4,20},{8,24},{12,28},{16,... | collective-permute-start | bytes 14 | tf_op jit(solution)/shard_map/cond/branch_2_fun/ppermute | solution.py:28
Sparse Core Ops, SparseCore 0:
  12.0 88.1 all-gather.2
  110.4 82.3 reduce-scatter.2
  198.0 85.0 all-gather.4
  293.3 82.3 reduce-scatter.4
where the time goes:
time: 502 us; the launch traced here: 501 us
  waiting for transfers between devices  347 us (69%)
  starting transfers between devices  90.5 us (18%)
  other arithmetic  23.3 us (5%)
  matrix products  20 us (4%)
  between operations  18.2 us (4%)
    all_gather x2, waiting for transfers between devices, per_device(): lax.all_gather(current, 'fsdp', axis=0, tiled=True)  171 us
    reduce_scatter x2, waiting for transfers between devices, per_device(): lax.psum_scatter(lax.dot_general(delta, normed, (((0,), (0,)), ((), ())),...  162 us
    ppermute x4, starting transfers between devices, shifted(): return lax.ppermute(block, axis, route)  90.3 us
    dot_general x2, matrix products, per_device(): lax.dot_general(delta, normed, (((0,), (0,)), ((), ())), preferred_elemen...  20 us
    ppermute x4, waiting for transfers between devices, shifted(): return lax.ppermute(block, axis, route)  12.6 us
  transfers between devices with their start and end apart: 8, of which 6 were waited for; matrix products, arithmetic and copies ran while one was open for 0% of the time, Pallas kernels for 0%

commit v1 on v0

v1 whole, which is shorter than its diff:
```python
from functools import partial
import math

import jax
import jax.numpy as jnp
from jax import lax
from jax.experimental import pallas as pl
from jax.experimental.pallas import tpu as pltpu
from jax.sharding import PartitionSpec as P

EXPONENTS = 3
CHUNKS = 2
RING = 4
TILE = 512
VMEM = 63 * 2**20

learning_rate = 0.5
epsilon = 1e-06


def swap(block, bit):
    n = lax.axis_size("fsdp")
    return lax.ppermute(block, "fsdp", [(i, i ^ bit) for i in range(n)])


def pushed(block, distance):
    n = lax.axis_size("gossip")
    return lax.ppermute(block, "gossip", [(i, (i + distance) % n) for i in range(n)])


def after(block, *earlier):
    return lax.optimization_barrier((block, *earlier))[0]


def norm_kernel(h_ref, out_ref):
    values = h_ref[0, 0].astype(jnp.float32)
    scale = lax.rsqrt(jnp.mean(values * values, axis=-1, keepdims=True) + epsilon)
    out_ref[...] = (values * scale).astype(jnp.bfloat16)


def normalized(hidden_in, step):
    _, _, n_tok, width = hidden_in.shape
    tile = 128
    return pl.pallas_call(
        norm_kernel,
        grid=(n_tok // tile,),
        in_specs=[pl.BlockSpec((1, 1, tile, width), lambda i: (step, 0, i, 0))],
        out_specs=pl.BlockSpec((tile, width), lambda i: (i, 0)),
        out_shape=jax.ShapeDtypeStruct((n_tok, width), jnp.bfloat16),
        compiler_params=pltpu.CompilerParams(vmem_limit_bytes=VMEM),
        name="normalize",
    )(hidden_in)


def copy_kernel(f_ref, t_ref, out_ref):
    out_ref[0] = t_ref[0, 0]


def packed(f, targets, n_rows, owners):
    steps, _, n_tok, _ = targets.shape
    return pl.pallas_call(
        copy_kernel,
        grid_spec=pltpu.PrefetchScalarGridSpec(
            num_scalar_prefetch=1,
            grid=(steps, len(owners)),
            in_specs=[
                pl.BlockSpec(
                    (1, 1, n_tok, n_rows), lambda s, o, f: (s, 0, 0, jnp.bitwise_xor(f[0], owners[0] + o))
                )
            ],
            out_specs=pl.BlockSpec((1, n_tok, n_rows), lambda s, o, f: (s, o, 0)),
        ),
        out_shape=jax.ShapeDtypeStruct((steps, len(owners) * n_tok, n_rows), jnp.bfloat16),
        compiler_params=pltpu.CompilerParams(vmem_limit_bytes=VMEM),
        name="pack_targets",
    )(f, targets)


def pair_kernel(last, w_ref, same_ref, f_ref, left_ref, n0, n1, t0, t1, rows_ref, *refs, step):
    deltas = refs[-1]
    width = left_ref.shape[1]
    root_width = math.sqrt(width)
    n_tok = n0.shape[0]

    @pl.when(pl.program_id(0) == 0)
    def _():
        scale = 2.0**step / (root_width * w_ref[0])
        for b, (n, t) in enumerate(((n0, t0), (n1, t1))):
            pre = scale * lax.dot_general(
                n[...], left_ref[...], (((1,), (1,)), ((), ())), preferred_element_type=jnp.float32
            )
            goal = t[...].reshape(t.shape[-2:]).astype(jnp.float32)
            sigma = jax.nn.sigmoid(pre)
            slope = sigma * (1.0 + pre * (1.0 - sigma))
            deltas[:, b * n_tok : (b + 1) * n_tok] = ((pre * sigma - goal) * slope).astype(jnp.bfloat16).T

    k = pl.ds(pl.multiple_of(pl.program_id(0) * TILE, TILE), TILE)
    total = jnp.dot(deltas[:, :n_tok], n0[:, k], preferred_element_type=jnp.float32)
    total += jnp.dot(deltas[:, n_tok:], n1[:, k], preferred_element_type=jnp.float32)
    rows = rows_ref[...] - (learning_rate / root_width) * total
    if not last:
        refs[0][...] = rows
        return
    halved_ref, first_ref, second_ref = refs[:3]
    halved = rows * 0.5
    halved_ref[...] = halved
    message = halved
    if step == 1:
        message = jnp.where(same_ref[0] != 0, left_ref[:, k].astype(jnp.float32) + halved, halved)
    message = message.astype(jnp.bfloat16)
    half = first_ref.shape[0]
    first_ref[...] = message[:half]
    second_ref[...] = message[half:]


def pair(step, last, weight, same, f, left, ns, ts, rows):
    n_tok, width = ns[0].shape
    n_rows = rows.shape[0]
    half = n_rows // CHUNKS

    def goal(t, i):
        if i is None:
            return pl.BlockSpec((1, 1, n_tok, n_rows), lambda j, w, s, f: (step, 0, 0, f[0]))
        return pl.BlockSpec((1, n_tok, n_rows), lambda j, w, s, f: (step, i, 0))

    whole = pl.BlockSpec((n_rows, width), lambda j, w, s, f: (0, 0))
    tile = pl.BlockSpec((n_rows, TILE), lambda j, w, s, f: (0, j))
    out_specs = [tile]
    out_shape = [jax.ShapeDtypeStruct((n_rows, width), jnp.float32)]
    if last:
        out_specs += [pl.BlockSpec((half, TILE), lambda j, w, s, f: (0, j))] * 2
        out_shape += [jax.ShapeDtypeStruct((half, width), jnp.bfloat16)] * 2
    return pl.pallas_call(
        partial(pair_kernel, last, step=step),
        grid_spec=pltpu.PrefetchScalarGridSpec(
            num_scalar_prefetch=3,
            grid=(width // TILE,),
            in_specs=[whole]
            + [pl.BlockSpec((n_tok, width), lambda j, w, s, f: (0, 0))] * 2
            + [goal(*t) for t in ts]
            + [tile],
            out_specs=out_specs,
            scratch_shapes=[pltpu.VMEM((n_rows, 2 * n_tok), jnp.bfloat16)],
        ),
        out_shape=out_shape,
        compiler_params=pltpu.CompilerParams(vmem_limit_bytes=VMEM),
        cost_estimate=pl.CostEstimate(flops=2**20, bytes_accessed=2**20, transcendentals=0),
        name="pair_of_blocks",
    )(weight, same, f, left, *ns, *(t for t, _ in ts), rows)


def sum_kernel(w_ref, *refs):
    source, arrived = refs[0], [refs[1 + 2 * c : 3 + 2 * c] for c in range(CHUNKS)]
    out, halved, first, second, in_sems, out_sems = refs[1 + 2 * CHUNKS :]
    bufs = (halved, first, second)
    count = halved.shape[0] // CHUNKS
    pieces = in_sems.shape[2]
    piece = count // pieces
    factor = 1.0 / w_ref[0]

    def part(c, i):
        return pl.ds(pl.multiple_of(c * count + i * piece, piece), piece)

    def copies_in(c, i):
        there = pl.ds(pl.multiple_of(i * piece, piece), piece)
        froms = [source.at[part(c, i)]] + [a.at[there] for a in arrived[c]]
        return [
            pltpu.make_async_copy(x, bufs[a].at[part(c, i)], in_sems.at[c, a, i]) for a, x in enumerate(froms)
        ]

    def copy_out(c, i):
        return pltpu.make_async_copy(halved.at[part(c, i)], out.at[part(c, i)], out_sems.at[c, i])

    def run(c, body):
        lax.fori_loop(0, pieces, lambda i, _: (body(c, i), 0)[1], 0)

    def start(c, i):
        for x in copies_in(c, i):
            x.start()

    def work(c, i):
        for x in copies_in(c, i):
            x.wait()

        def strip(j, _):
            s = pl.ds(pl.multiple_of(c * count + i * piece + j * 16, 16), 16)
            halved[s] = (halved[s] + first[s].astype(jnp.float32) + second[s].astype(jnp.float32)) * factor
            return 0

        lax.fori_loop(0, piece // 16, strip, 0)
        copy_out(c, i).start()

    for c in range(CHUNKS):
        run(c, start)
    for c in range(CHUNKS):
        run(c, work)
    for c in range(CHUNKS):
        run(c, lambda c, i: copy_out(c, i).wait())


def divided(weight, halved, first, second):
    n_rows, width = halved.shape
    pieces = 4
    operands = [halved] + [x for chunk in zip(first, second) for x in chunk]
    anywhere = pl.BlockSpec(memory_space=pl.ANY)
    return pl.pallas_call(
        sum_kernel,
        grid_spec=pltpu.PrefetchScalarGridSpec(
            num_scalar_prefetch=1,
            grid=(),
            in_specs=[anywhere] * len(operands),
            out_specs=anywhere,
            scratch_shapes=[
                pltpu.VMEM((n_rows, width), jnp.float32),
                pltpu.VMEM((n_rows, width), jnp.bfloat16),
                pltpu.VMEM((n_rows, width), jnp.bfloat16),
                pltpu.SemaphoreType.DMA((CHUNKS, 3, pieces)),
                pltpu.SemaphoreType.DMA((CHUNKS, pieces)),
            ],
        ),
        out_shape=jax.ShapeDtypeStruct((n_rows, width), jnp.float32),
        compiler_params=pltpu.CompilerParams(vmem_limit_bytes=VMEM),
        name="last_sum",
    )(weight, *operands)


def along(block, distance):
    n = lax.axis_size("gossip")
    return lax.ppermute(block, "gossip", [(i, i - i % RING + (i + distance) % RING) for i in range(n)])


def across(block, wrapped):
    n = lax.axis_size("gossip")
    return lax.ppermute(block, "gossip", [(i, (i + RING) % n if i % RING in wrapped else i) for i in range(n)])


def exchange(k0, k1, m0, m1):
    if k0 == k1:
        return [jnp.zeros_like(m) for m in m0], [pushed(m, 1 << k1) for m in m1]
    begun = []
    for k, m in ((k0, m0), (k1, m1)):
        d = 1 << k
        if d < RING:
            begun.append([along(m[0], d), across(m[1], range(RING - d, RING))])
        else:
            begun.append([pushed(x, d) for x in m])
    sent = []
    for k, m in zip((k0, k1), begun):
        d = 1 << k
        sent.append([across(m[0], range(d)), along(m[1], d)] if d < RING else m)
    return sent[0], sent[1]


def per_device(numerator, push_weight, hidden_in, targets, exponents):
    numerators = numerator[0]
    n_rows, width = numerators.shape
    weight = push_weight.astype(jnp.float32)
    same = (exponents[0] == exponents[1]).astype(jnp.int32)[None]
    f = lax.axis_index("fsdp").astype(jnp.int32)[None]

    own0 = normalized(hidden_in, 0)
    chip0 = swap(own0, 2)
    t_chip_out = packed(f, targets, n_rows, (2, 3))
    t_chip = swap(t_chip_out, 2)
    own1 = normalized(after(hidden_in, t_chip_out), 1)
    chip1 = swap(own1, 2)

    t_core_out = packed(after(f, own1), targets, n_rows, (1,))
    received = []
    tile = jnp.broadcast_to(push_weight, (16, 128))
    for k in range(EXPONENTS):
        tile = after(tile, t_core_out, *received)
        received.append(pushed(tile, 1 << k))
    received = [x[0, :1].astype(jnp.float32) for x in received]

    def chosen(k):
        return jnp.where(k == 0, received[0], jnp.where(k == 1, received[1], received[2]))

    weight_out = (weight * 0.25 + chosen(exponents[0]) * 0.5) + chosen(exponents[1]) * 0.25

    current0 = after(numerators, own1).astype(jnp.bfloat16)
    chip0 = after(chip0, current0, weight_out)
    core0 = swap(after(own0, chip0), 1)
    core1 = swap(after(own1, chip0), 1)
    t_core = swap(after(t_core_out, chip0), 1)
    corner0 = swap(chip0, 1)
    t_corner = swap(t_chip, 1)
    t_near = [(targets, None), (t_core, 0)]
    t_far = [(t_chip, 0), (t_corner, 1)]
    [rows0] = pair(0, False, weight, same, f, current0, [own0, core0], t_near, numerators)
    halved0, *m0 = pair(0, True, weight, same, f, current0, [chip0, corner0], t_far, rows0)
    left1 = jnp.concatenate(m0, axis=0)
    [rows1] = pair(1, False, weight, same, f, left1, [own1, core1], t_near, halved0)
    chip1 = after(chip1, rows1)
    halved1, *m1 = pair(1, True, weight, same, f, left1, [chip1, swap(chip1, 1)], t_far, rows1)

    branches = [partial(exchange, k0, k1) for k0 in range(EXPONENTS) for k1 in range(EXPONENTS)]
    a0, a1 = lax.switch(exponents[0] * EXPONENTS + exponents[1], branches, m0, m1)
    return divided(weight_out, halved1, a0, a1)[None], weight_out


def solution(mesh):
    in_specs = (
        P("gossip", "fsdp", None),
        P("gossip"),
        P(None, "gossip", "fsdp", None),
        P(None, "gossip", "fsdp", None),
        P(),
    )
    out_specs = (P("gossip", "fsdp", None), P("gossip"))
    return jax.shard_map(
        per_device, mesh=mesh, in_specs=in_specs, out_specs=out_specs, check_vma=False
    )
```

time: 502 us -> 210 us (0.42)
  waiting for transfers between devices: 347 us -> 95.2 us
  starting transfers between devices: 90.5 us -> 31.3 us
  Pallas kernels: 0 us -> 50.8 us
  matrix products: 20 us -> 0 us
  other arithmetic: 23.3 us -> 3.99 us
  loops' own time: 0.04 us -> 8.69 us
  between operations: 18.2 us -> 11.8 us
    all_gather x2 -> x0, waiting for transfers between devices: 171 us -> none  [per_device(): lax.all_gather(current, 'fsdp', axis=0, tiled=True)]
    reduce_scatter x2 -> x0, waiting for transfers between devices: 162 us -> none  [per_device(): lax.psum_scatter(lax.dot_general(delta, normed, (((0,), (0,)), ((), ())),...]
    ppermute x4 -> x20, waiting for transfers between devices: 12.6 us -> 95.2 us  [the longest x4 59.7 us: along(): lax.ppermute(block, 'gossip', [(i, i - i % RING + (i + distance) % RING)...]
    ppermute x4 -> x20, starting transfers between devices: 90.3 us -> 31.3 us  [the longest x9 10.5 us: swap(): return lax.ppermute(block, 'fsdp', [(i, i ^ bit) for i in range(n)])]
    pallas_call x0 -> x9, Pallas kernels: none -> 50.8 us  [the longest x4 35.6 us: pair(): pl.pallas_call(partial(pair_kernel, last, step=step), grid_spec=pltpu.Pre...]
    dot_general x2 -> x0, matrix products: 20 us -> none  [per_device(): lax.dot_general(delta, normed, (((0,), (0,)), ((), ())), preferred_elemen...]
    convert_element_type x3 -> x1, other arithmetic: 14.7 us -> 3.99 us  [per_device(): current0 = after(numerators, own1).astype(jnp.bfloat16)]
    another operation x0 -> x1, loops' own time: none -> 8.69 us  [per_device(): lax.switch(exponents[0] * EXPONENTS + exponents[1], branches, m0, m1)]
  transfers between devices with their start and end apart: 8 -> 20, of which waited for: 6 -> 9; matrix products, arithmetic and copies ran while one was open for 0% -> 5% of each run, Pallas kernels for 0% -> 16%
where the time goes in v1:
time: 210 us; the launch traced here: 209 us
  waiting for transfers between devices  95.2 us (45%)
  Pallas kernels  50.8 us (24%)
  starting transfers between devices  31.3 us (15%)
  between operations  11.8 us (6%)
  loops' own time  8.69 us (4%)
  local copies, waits for them, and re-layouts  6.88 us (3%)
  other arithmetic  3.99 us (2%)
    ppermute x4, waiting for transfers between devices, along(): lax.ppermute(block, 'gossip', [(i, i - i % RING + (i + distance) % RING)...  59.7 us
    pallas_call x4, Pallas kernels, pair(): pl.pallas_call(partial(pair_kernel, last, step=step), grid_spec=pltpu.Pre...  35.6 us
    ppermute x3, waiting for transfers between devices, pushed(): lax.ppermute(block, 'gossip', [(i, (i + distance) % n) for i in range(n)])  18.9 us
    ppermute x4, waiting for transfers between devices, across(): lax.ppermute(block, 'gossip', [(i, (i + RING) % n if i % RING in wrapped...  15.3 us
    ppermute x9, starting transfers between devices, swap(): return lax.ppermute(block, 'fsdp', [(i, i ^ bit) for i in range(n)])  10.5 us
    ppermute x4, starting transfers between devices, across(): lax.ppermute(block, 'gossip', [(i, (i + RING) % n if i % RING in wrapped...  10.2 us
    ppermute x4, starting transfers between devices, along(): lax.ppermute(block, 'gossip', [(i, i - i % RING + (i + distance) % RING)...  9.17 us
    another operation x1, loops' own time, per_device(): lax.switch(exponents[0] * EXPONENTS + exponents[1], branches, m0, m1)  8.69 us
  transfers between devices with their start and end apart: 20, of which 9 were waited for; matrix products, arithmetic and copies ran while one was open for 5% of the time, Pallas kernels for 16%

profile of v1, /device:TPU:1, one launch (start us, length us, event | category | flops | bytes accessed | tf_op | source)
XLA Modules:
  0.0 208.6 jit_solution(12113987269722616507)
XLA Ops:
  0.6 2.3 %normalize.3.n0 = bf16[256,2048]{1,0:T(8,128)(2,1)} custom-call(bf16[2,1,256,2048]{3,2,1,0:T(8,128)(2,1)} %h_ref.2), custom_call_target="tpu_custom_call" | custom-call | tf_op jit(solution)/shard_map/normalize/pallas_call | solution.py:44
  2.9 2.1 %collective-permute-start.49 = (bf16[256,2048]{1,0:T(8,128)(2,1)}, bf16[256,2048]{1,0:T(8,128)(2,1)}, u32[]{:S(2)}, u32[]{:S(2)}) collective-permute-start(bf16[256,2048]{1,0:T(8,128)(2,1)} %normalize.3.n0), channel_id=1, source_target_pairs={{0,2},{1,3},{2,0},{3,1},{4,6},{5,7},{6,4},{7,5},{8,10},{9,11},{10,... | collective-permute-start | bytes 3145736 | tf_op jit(solution)/shard_map/ppermute | solution.py:23
  5.1 3.4 %pack_targets.2 = bf16[2,512,512]{2,1,0:T(8,128)(2,1)} custom-call(s32[1]{0:T(128)} %bitcast.3.f_ref, bf16[2,1,256,2048]{3,2,1,0:T(8,128)(2,1)} %t0.3), custom_call_target="tpu_custom_call" | custom-call | tf_op jit(solution)/shard_map/pack_targets/pallas_call | solution.py:61
  8.4 0.0 collective-permute-start.51
  8.4 2.2 %normalize.2.n0 = bf16[256,2048]{1,0:T(8,128)(2,1)} custom-call(bf16[2,1,256,2048]{3,2,1,0:T(8,128)(2,1)} %h_ref.2), custom_call_target="tpu_custom_call" | custom-call | tf_op jit(solution)/shard_map/normalize/pallas_call | solution.py:44
  10.7 1.8 pack_targets.3
  13.1 1.5 collective-permute-start.46
  14.6 10.3 %collective-permute-done.46 = bf16[16,128]{1,0:T(8,128)(2,1)S(1)} collective-permute-done((bf16[16,128]{1,0:T(8,128)(2,1)S(1)}, bf16[16,128]{1,0:T(8,128)(2,1)S(1)}, u32[]{:S(2)}, u32[]{:S(2)}) %collective-permute-start.46) | collective-permute-done | bytes 4128 | tf_op jit(solution)/shard_map/ppermute | solution.py:28
  24.9 0.0 collective-permute-start.47
  24.9 8.6 %collective-permute-done.47 = bf16[16,128]{1,0:T(8,128)(2,1)S(1)} collective-permute-done((bf16[16,128]{1,0:T(8,128)(2,1)S(1)}, bf16[16,128]{1,0:T(8,128)(2,1)S(1)}, u32[]{:S(2)}, u32[]{:S(2)}) %collective-permute-start.47) | collective-permute-done | bytes 4128 | tf_op jit(solution)/shard_map/ppermute | solution.py:28
  33.5 0.0 collective-permute-start.48
  33.5 0.0 copy-done.5
  33.5 0.7 fusion
  36.7 0.0 copy-start.4
  36.7 0.0 copy-start
  36.8 4.0 %convert_element_type.32.left_ref = bf16[512,2048]{1,0:T(8,128)(2,1)} convert(f32[512,2048]{1,0:T(8,128)} %bitcast.18) | non-fusion elementwise | flops 1048576 | bytes 6291456 | tf_op jit(solution)/shard_map/convert_element_type | solution.py:281
  40.7 0.5 slice.24
  41.3 0.6 slice.25
  41.9 0.0 collective-permute-done.48
  41.9 0.6 slice.26
  46.3 0.0 collective-permute-done.49.n0
  46.4 0.0 copy-done.4
  46.4 3.3 %collective-permute-start.54 = (bf16[2,256,512]{2,1,0:T(8,128)(2,1)S(1)}, bf16[2,256,512]{2,1,0:T(8,128)(2,1)S(1)}, u32[]{:S(2)}, u32[]{:S(2)}) collective-permute-start(bf16[2,256,512]{2,1,0:T(8,128)(2,1)S(1)} %copy-done.4), channel_id=1, source_target_pairs={{0,1},{1,0},{2,3},{3,2},{4,5},{5,4},{6,7},{7,6},{8,9},{9,8},{10,11... | collective-permute-start | bytes 1572872 | tf_op jit(solution)/shard_map/ppermute | solution.py:23
  49.7 0.0 copy-done
  49.7 0.1 collective-permute-start.53
  49.8 0.4 collective-permute-start.50
  50.2 0.0 collective-permute-done.51.t0
  50.2 2.0 collective-permute-start.52
  52.2 0.0 collective-permute-start.56
  52.2 0.0 collective-permute-done.54.t1
  52.2 1.8 collective-permute-start.55
  55.4 0.0 collective-permute-done.53.n1
  55.4 0.0 copy-start.2
  55.4 1.0 copy-done.2
  56.4 8.6 %pair_of_blocks.4.rows_ref = f32[512,2048]{1,0:T(8,128)} custom-call(f32[1]{0:T(128)S(6)} %convert_element_type.25.w_ref, s32[1]{0:T(128)} %bitcast.14.same_ref, s32[1]{0:T(128)} %bitcast.3.f_ref, bf16[512,2048]{1,0:T(8,128)(2,1)} %convert_element_type.32.left_ref, bf16[256,2048]{1,0:T(8,128)(2,1)} %normalize.3.n0, bf16[256,2048]{1,0:T(8,128)(2,1)} %copy-done.2, ...), custom_call_target="tpu_custom_call" | custom-call | flops 1048576 | bytes 1048576 | tf_op jit(solution)/shard_map/pair_of_blocks/pallas_call | solution.py:133
  65.0 0.0 collective-permute-done.50.n1
  65.0 0.0 collective-permute-done.52.t1
  65.0 9.2 %pair_of_blocks.5 = (f32[512,2048]{1,0:T(8,128)}, bf16[256,2048]{1,0:T(8,128)(2,1)}, bf16[256,2048]{1,0:T(8,128)(2,1)}) custom-call(f32[1]{0:T(128)S(6)} %convert_element_type.25.w_ref, s32[1]{0:T(128)} %bitcast.14.same_ref, s32[1]{0:T(128)} %bitcast.3.f_ref, bf16[512,2048]{1,0:T(8,128)(2,1)} %convert_element_type.32.left_ref, ...), custom_call_target="tpu_custom_call" | custom-call | flops 1048576 | bytes 1048576 | tf_op jit(solution)/shard_map/pair_of_blocks/pallas_call | solution.py:133
  74.2 2.4 %constant_dynamic-update-slice_fusion.1 = bf16[512,2048]{1,0:T(8,128)(2,1)} fusion(bf16[256,2048]{1,0:T(8,128)(2,1)} %get-tuple-element.122), kind=kLoop, calls=%fused_computation.1 | loop fusion | bytes 2097152
  76.6 1.1 constant_dynamic-update-slice_fusion.left_ref
  77.7 0.0 collective-permute-done.56.n1
  77.7 8.6 %pair_of_blocks.6.rows_ref = f32[512,2048]{1,0:T(8,128)} custom-call(f32[1]{0:T(128)S(6)} %convert_element_type.25.w_ref, s32[1]{0:T(128)} %bitcast.14.same_ref, s32[1]{0:T(128)} %bitcast.3.f_ref, bf16[512,2048]{1,0:T(8,128)(2,1)} %constant_dynamic-update-slice_fusion.left_ref, bf16[256,2048]{1,0:T(8,128)(2,1)} %normalize.2.n0, ...), custom_call_target="tpu_custom_call" | custom-call | flops 1048576 | bytes 1048576 | tf_op jit(solution)/shard_map/pair_of_blocks/pallas_call | solution.py:133
  86.3 0.0 collective-permute-done.55.n0
  86.3 0.7 collective-permute-start.57
  88.3 1.3 collective-permute-done.57.n1
  89.6 9.2 %pair_of_blocks.7 = (f32[512,2048]{1,0:T(8,128)}, bf16[256,2048]{1,0:T(8,128)(2,1)}, bf16[256,2048]{1,0:T(8,128)(2,1)}) custom-call(f32[1]{0:T(128)S(6)} %convert_element_type.25.w_ref, s32[1]{0:T(128)} %bitcast.14.same_ref, s32[1]{0:T(128)} %bitcast.3.f_ref, bf16[512,2048]{1,0:T(8,128)(2,1)} %constant_dynamic-update-slice_fusion.left_ref, ...), custom_call_target="tpu_custom_call" | custom-call | flops 1048576 | bytes 1048576 | tf_op jit(solution)/shard_map/pair_of_blocks/pallas_call | solution.py:133
  98.8 103.0 %conditional.1 = (bf16[256,2048]{1,0:T(8,128)(2,1)}, bf16[256,2048]{1,0:T(8,128)(2,1)}, bf16[256,2048]{1,0:T(8,128)(2,1)}, bf16[256,2048]{1,0:T(8,128)(2,1)}) conditional(s32[]{:T(128)} %clamp.3, (bf16[256,2048]{1,0:T(8,128)(2,1)}, bf16[256,2048]{1,0:T(8,128)(2,1)}) %tuple.66, (bf16[256,2048]{1,0:T(8,128)(2,1)}, ...), branch_computations={%region_0.1_spmd, %region_1.2_spmd, %region_2.3_spmd, %region_3.4_... | conditional | bytes 33554784 | solution.py:298
  98.8 2.6 %collective-permute-start.16 = (bf16[256,2048]{1,0:T(8,128)(2,1)}, bf16[256,2048]{1,0:T(8,128)(2,1)S(1)}, u32[]{:S(2)}, u32[]{:S(2)}) collective-permute-start(bf16[256,2048]{1,0:T(8,128)(2,1)} %get-tuple-element.70), channel_id=1, source_target_pairs={{0,8},{4,12},{8,0},{12,4},{16,24},{20,28},{24,16},{28,20},{32,40},... | collective-permute-start | bytes 3145736 | tf_op jit(solution)/shard_map/cond/branch_3_fun/ppermute | solution.py:229
  101.4 1.9 collective-permute-start.18
  103.2 0.3 collective-permute-start.20
  103.5 1.9 collective-permute-start.22
  105.4 19.5 %collective-permute-done.16 = bf16[256,2048]{1,0:T(8,128)(2,1)S(1)} collective-permute-done((bf16[256,2048]{1,0:T(8,128)(2,1)}, bf16[256,2048]{1,0:T(8,128)(2,1)S(1)}, u32[]{:S(2)}, u32[]{:S(2)}) %collective-permute-start.16) | collective-permute-done | bytes 1048608 | tf_op jit(solution)/shard_map/cond/branch_3_fun/ppermute | solution.py:229
  124.9 3.3 %collective-permute-start.17 = (bf16[256,2048]{1,0:T(8,128)(2,1)S(1)}, bf16[256,2048]{1,0:T(8,128)(2,1)}, u32[]{:S(2)}, u32[]{:S(2)}) collective-permute-start(bf16[256,2048]{1,0:T(8,128)(2,1)S(1)} %collective-permute-done.16), channel_id=1, source_target_pairs={{0,16},{4,20},{8,8},{12,12},{16,32},{20,36},{24,24},{28,28},{32,48... | collective-permute-start | bytes 3145736 | tf_op jit(solution)/shard_map/cond/branch_3_fun/ppermute | solution.py:234
  128.2 0.0 collective-permute-done.18
  128.2 6.2 %collective-permute-start.19 = (bf16[256,2048]{1,0:T(8,128)(2,1)S(1)}, bf16[256,2048]{1,0:T(8,128)(2,1)}, u32[]{:S(2)}, u32[]{:S(2)}) collective-permute-start(bf16[256,2048]{1,0:T(8,128)(2,1)S(1)} %collective-permute-done.18), channel_id=1, source_target_pairs={{0,8},{4,12},{8,0},{12,4},{16,24},{20,28},{24,16},{28,20},{32,40},... | collective-permute-start | bytes 3145736 | tf_op jit(solution)/shard_map/cond/branch_3_fun/ppermute | solution.py:229
  134.4 14.4 %collective-permute-done.20 = bf16[256,2048]{1,0:T(8,128)(2,1)S(1)} collective-permute-done((bf16[256,2048]{1,0:T(8,128)(2,1)}, bf16[256,2048]{1,0:T(8,128)(2,1)S(1)}, u32[]{:S(2)}, u32[]{:S(2)}) %collective-permute-start.20) | collective-permute-done | bytes 1048608 | tf_op jit(solution)/shard_map/cond/branch_3_fun/ppermute | solution.py:229
  148.8 3.2 %collective-permute-start.21 = (bf16[256,2048]{1,0:T(8,128)(2,1)S(1)}, bf16[256,2048]{1,0:T(8,128)(2,1)}, u32[]{:S(2)}, u32[]{:S(2)}) collective-permute-start(bf16[256,2048]{1,0:T(8,128)(2,1)S(1)} %collective-permute-done.20), channel_id=1, source_target_pairs={{0,16},{4,4},{8,8},{12,12},{16,32},{20,20},{24,24},{28,28},{32,48}... | collective-permute-start | bytes 3145736 | tf_op jit(solution)/shard_map/cond/branch_3_fun/ppermute | solution.py:234
  152.0 0.0 collective-permute-done.22
  152.0 0.1 collective-permute-start.23
  152.1 3.9 %collective-permute-done.17 = bf16[256,2048]{1,0:T(8,128)(2,1)} collective-permute-done((bf16[256,2048]{1,0:T(8,128)(2,1)S(1)}, bf16[256,2048]{1,0:T(8,128)(2,1)}, u32[]{:S(2)}, u32[]{:S(2)}) %collective-permute-start.17) | collective-permute-done | bytes 1048608 | tf_op jit(solution)/shard_map/cond/branch_3_fun/ppermute | solution.py:234
  156.0 14.0 %collective-permute-done.19 = bf16[256,2048]{1,0:T(8,128)(2,1)} collective-permute-done((bf16[256,2048]{1,0:T(8,128)(2,1)S(1)}, bf16[256,2048]{1,0:T(8,128)(2,1)}, u32[]{:S(2)}, u32[]{:S(2)}) %collective-permute-start.19) | collective-permute-done | bytes 1048608 | tf_op jit(solution)/shard_map/cond/branch_3_fun/ppermute | solution.py:229
  170.0 11.3 %collective-permute-done.21 = bf16[256,2048]{1,0:T(8,128)(2,1)} collective-permute-done((bf16[256,2048]{1,0:T(8,128)(2,1)S(1)}, bf16[256,2048]{1,0:T(8,128)(2,1)}, u32[]{:S(2)}, u32[]{:S(2)}) %collective-permute-start.21) | collective-permute-done | bytes 1048608 | tf_op jit(solution)/shard_map/cond/branch_3_fun/ppermute | solution.py:234
  181.3 11.8 %collective-permute-done.23 = bf16[256,2048]{1,0:T(8,128)(2,1)} collective-permute-done((bf16[256,2048]{1,0:T(8,128)(2,1)S(1)}, bf16[256,2048]{1,0:T(8,128)(2,1)}, u32[]{:S(2)}, u32[]{:S(2)}) %collective-permute-start.23) | collective-permute-done | bytes 1048608 | tf_op jit(solution)/shard_map/cond/branch_3_fun/ppermute | solution.py:229
  201.8 5.5 %last_sum.1 = f32[512,2048]{1,0:T(8,128)} custom-call(f32[1]{0:T(128)} %add.10.w_ref, f32[512,2048]{1,0:T(8,128)} %get-tuple-element.127.refs_0_, bf16[256,2048]{1,0:T(8,128)(2,1)} %get-tuple-element.130.refs_1_, bf16[256,2048]{1,0:T(8,128)(2,1)} %get-tuple-element.131.refs_2_, bf16[256,2048]{1,0:T(8,128)(2,1)} %get-tuple-element.132.refs_3_, ...), custom_call_target="tpu_custom_call" | custom-call | tf_op jit(solution)/shard_map/last_sum/pallas_call | solution.py:206
  (6 shorter events, 0.0 us)
Async XLA Ops:
  2.9 43.4 %collective-permute-start.49 = (bf16[256,2048]{1,0:T(8,128)(2,1)}, bf16[256,2048]{1,0:T(8,128)(2,1)}, u32[]{:S(2)}, u32[]{:S(2)}) collective-permute-start(bf16[256,2048]{1,0:T(8,128)(2,1)} %normalize.3.n0), channel_id=1, source_target_pairs={{0,2},{1,3},{2,0},{3,1},{4,6},{5,7},{6,4},{7,5},{8,10},{9,11},{10,... | collective-permute-start | bytes 3145736 | tf_op jit(solution)/shard_map/ppermute | solution.py:23
  8.4 41.8 %collective-permute-start.51 = (bf16[2,512,512]{2,1,0:T(8,128)(2,1)}, bf16[2,512,512]{2,1,0:T(8,128)(2,1)}, u32[]{:S(2)}, u32[]{:S(2)}) collective-permute-start(bf16[2,512,512]{2,1,0:T(8,128)(2,1)} %pack_targets.2), channel_id=1, source_target_pairs={{0,2},{1,3},{2,0},{3,1},{4,6},{5,7},{6,4},{7,5},{8,10},{9,11},{10,... | collective-permute-start | bytes 3145736 | tf_op jit(solution)/shard_map/ppermute | solution.py:23
  10.7 22.8 %copy-start.5 = (s32[2]{0:T(128)S(1)}, s32[2]{0:T(128)}, u32[]{:S(2)}) copy-start(s32[2]{0:T(128)} %param.18) | copy-start | bytes 28
  13.1 11.7 %collective-permute-start.46 = (bf16[16,128]{1,0:T(8,128)(2,1)S(1)}, bf16[16,128]{1,0:T(8,128)(2,1)S(1)}, u32[]{:S(2)}, u32[]{:S(2)}) collective-permute-start(bf16[16,128]{1,0:T(8,128)(2,1)S(1)} %broadcast_in_dim.16), channel_id=1, source_target_pairs={{0,4},{4,8},{8,12},{12,16},{16,20},{20,24},{24,28},{28,32},{32,36}... | collective-permute-start | bytes 12296 | tf_op jit(solution)/shard_map/ppermute | solution.py:28
  24.9 8.6 %collective-permute-start.47 = (bf16[16,128]{1,0:T(8,128)(2,1)S(1)}, bf16[16,128]{1,0:T(8,128)(2,1)S(1)}, u32[]{:S(2)}, u32[]{:S(2)}) collective-permute-start(bf16[16,128]{1,0:T(8,128)(2,1)S(1)} %broadcast_in_dim.16), channel_id=1, source_target_pairs={{0,8},{4,12},{8,16},{12,20},{16,24},{20,28},{24,32},{28,36},{32,40... | collective-permute-start | bytes 12296 | tf_op jit(solution)/shard_map/ppermute | solution.py:28
  33.5 8.4 %collective-permute-start.48 = (bf16[16,128]{1,0:T(8,128)(2,1)S(1)}, bf16[16,128]{1,0:T(8,128)(2,1)S(1)}, u32[]{:S(2)}, u32[]{:S(2)}) collective-permute-start(bf16[16,128]{1,0:T(8,128)(2,1)S(1)} %broadcast_in_dim.16), channel_id=1, source_target_pairs={{0,16},{4,20},{8,24},{12,28},{16,32},{20,36},{24,40},{28,44},{32,4... | collective-permute-start | bytes 12296 | tf_op jit(solution)/shard_map/ppermute | solution.py:28
  36.7 9.6 %copy-start.4 = (bf16[2,256,512]{2,1,0:T(8,128)(2,1)S(1)}, bf16[2,256,512]{2,1,0:T(8,128)(2,1)}, u32[]{:S(2)}) copy-start(bf16[2,256,512]{2,1,0:T(8,128)(2,1)} %pack_targets.3) | copy-start | bytes 1572868
  36.7 13.0 %copy-start = (bf16[256,2048]{1,0:T(8,128)(2,1)S(1)}, bf16[256,2048]{1,0:T(8,128)(2,1)}, u32[]{:S(2)}) copy-start(bf16[256,2048]{1,0:T(8,128)(2,1)} %normalize.3.n0) | copy-start | bytes 3145732
  46.4 5.9 %collective-permute-start.54 = (bf16[2,256,512]{2,1,0:T(8,128)(2,1)S(1)}, bf16[2,256,512]{2,1,0:T(8,128)(2,1)S(1)}, u32[]{:S(2)}, u32[]{:S(2)}) collective-permute-start(bf16[2,256,512]{2,1,0:T(8,128)(2,1)S(1)} %copy-done.4), channel_id=1, source_target_pairs={{0,1},{1,0},{2,3},{3,2},{4,5},{5,4},{6,7},{7,6},{8,9},{9,8},{10,11... | collective-permute-start | bytes 1572872 | tf_op jit(solution)/shard_map/ppermute | solution.py:23
  49.7 5.6 %collective-permute-start.53 = (bf16[256,2048]{1,0:T(8,128)(2,1)S(1)}, bf16[256,2048]{1,0:T(8,128)(2,1)S(1)}, u32[]{:S(2)}, u32[]{:S(2)}) collective-permute-start(bf16[256,2048]{1,0:T(8,128)(2,1)S(1)} %copy-done), channel_id=1, source_target_pairs={{0,1},{1,0},{2,3},{3,2},{4,5},{5,4},{6,7},{7,6},{8,9},{9,8},{10,11... | collective-permute-start | bytes 3145736 | tf_op jit(solution)/shard_map/ppermute | solution.py:23
  49.8 15.2 %collective-permute-start.50 = (bf16[256,2048]{1,0:T(8,128)(2,1)}, bf16[256,2048]{1,0:T(8,128)(2,1)}, u32[]{:S(2)}, u32[]{:S(2)}) collective-permute-start(bf16[256,2048]{1,0:T(8,128)(2,1)} %collective-permute-done.49.n0), channel_id=1, source_target_pairs={{0,1},{1,0},{2,3},{3,2},{4,5},{5,4},{6,7},{7,6},{8,9},{9,8},{10,11... | collective-permute-start | bytes 3145736 | tf_op jit(solution)/shard_map/ppermute | solution.py:23
  50.2 14.8 %collective-permute-start.52 = (bf16[2,512,512]{2,1,0:T(8,128)(2,1)}, bf16[2,512,512]{2,1,0:T(8,128)(2,1)}, u32[]{:S(2)}, u32[]{:S(2)}) collective-permute-start(bf16[2,512,512]{2,1,0:T(8,128)(2,1)} %collective-permute-done.51.t0), channel_id=1, source_target_pairs={{0,1},{1,0},{2,3},{3,2},{4,5},{5,4},{6,7},{7,6},{8,9},{9,8},{10,11... | collective-permute-start | bytes 3145736 | tf_op jit(solution)/shard_map/ppermute | solution.py:23
  52.2 25.5 %collective-permute-start.56 = (bf16[256,2048]{1,0:T(8,128)(2,1)}, bf16[256,2048]{1,0:T(8,128)(2,1)}, u32[]{:S(2)}, u32[]{:S(2)}) collective-permute-start(bf16[256,2048]{1,0:T(8,128)(2,1)} %normalize.2.n0), channel_id=1, source_target_pairs={{0,1},{1,0},{2,3},{3,2},{4,5},{5,4},{6,7},{7,6},{8,9},{9,8},{10,11... | collective-permute-start | bytes 3145736 | tf_op jit(solution)/shard_map/ppermute | solution.py:23
  52.2 4.2 %copy-start.1 = (bf16[2,256,512]{2,1,0:T(8,128)(2,1)}, bf16[2,256,512]{2,1,0:T(8,128)(2,1)S(1)}, u32[]{:S(2)}) copy-start(bf16[2,256,512]{2,1,0:T(8,128)(2,1)S(1)} %collective-permute-done.54.t1) | copy-start | bytes 1572868
  52.2 34.1 %collective-permute-start.55 = (bf16[256,2048]{1,0:T(8,128)(2,1)}, bf16[256,2048]{1,0:T(8,128)(2,1)}, u32[]{:S(2)}, u32[]{:S(2)}) collective-permute-start(bf16[256,2048]{1,0:T(8,128)(2,1)} %normalize.2.n0), channel_id=1, source_target_pairs={{0,2},{1,3},{2,0},{3,1},{4,6},{5,7},{6,4},{7,5},{8,10},{9,11},{10,... | collective-permute-start | bytes 3145736 | tf_op jit(solution)/shard_map/ppermute | solution.py:23
  55.4 1.0 copy-start.2
  74.2 2.4 %copy-start.3 = (bf16[256,2048]{1,0:T(8,128)(2,1)S(1)}, bf16[256,2048]{1,0:T(8,128)(2,1)}, u32[]{:S(2)}) copy-start(bf16[256,2048]{1,0:T(8,128)(2,1)} %get-tuple-element.123) | copy-start | bytes 3145732
  86.3 3.3 %collective-permute-start.57 = (bf16[256,2048]{1,0:T(8,128)(2,1)}, bf16[256,2048]{1,0:T(8,128)(2,1)}, u32[]{:S(2)}, u32[]{:S(2)}) collective-permute-start(bf16[256,2048]{1,0:T(8,128)(2,1)} %collective-permute-done.55.n0), channel_id=1, source_target_pairs={{0,1},{1,0},{2,3},{3,2},{4,5},{5,4},{6,7},{7,6},{8,9},{9,8},{10,11... | collective-permute-start | bytes 3145736 | tf_op jit(solution)/shard_map/ppermute | solution.py:23
  98.8 26.1 %collective-permute-start.16 = (bf16[256,2048]{1,0:T(8,128)(2,1)}, bf16[256,2048]{1,0:T(8,128)(2,1)S(1)}, u32[]{:S(2)}, u32[]{:S(2)}) collective-permute-start(bf16[256,2048]{1,0:T(8,128)(2,1)} %get-tuple-element.70), channel_id=1, source_target_pairs={{0,8},{4,12},{8,0},{12,4},{16,24},{20,28},{24,16},{28,20},{32,40},... | collective-permute-start | bytes 3145736 | tf_op jit(solution)/shard_map/cond/branch_3_fun/ppermute | solution.py:229
  101.4 26.8 %collective-permute-start.18 = (bf16[256,2048]{1,0:T(8,128)(2,1)}, bf16[256,2048]{1,0:T(8,128)(2,1)S(1)}, u32[]{:S(2)}, u32[]{:S(2)}) collective-permute-start(bf16[256,2048]{1,0:T(8,128)(2,1)} %get-tuple-element.71), channel_id=1, source_target_pairs={{0,0},{4,4},{8,24},{12,28},{16,16},{20,20},{24,40},{28,44},{32,32}... | collective-permute-start | bytes 3145736 | tf_op jit(solution)/shard_map/cond/branch_3_fun/ppermute | solution.py:234
  103.2 45.6 %collective-permute-start.20 = (bf16[256,2048]{1,0:T(8,128)(2,1)}, bf16[256,2048]{1,0:T(8,128)(2,1)S(1)}, u32[]{:S(2)}, u32[]{:S(2)}) collective-permute-start(bf16[256,2048]{1,0:T(8,128)(2,1)} %get-tuple-element.72), channel_id=1, source_target_pairs={{0,4},{4,8},{8,12},{12,0},{16,20},{20,24},{24,28},{28,16},{32,36},... | collective-permute-start | bytes 3145736 | tf_op jit(solution)/shard_map/cond/branch_3_fun/ppermute | solution.py:229
  103.5 48.5 %collective-permute-start.22 = (bf16[256,2048]{1,0:T(8,128)(2,1)}, bf16[256,2048]{1,0:T(8,128)(2,1)S(1)}, u32[]{:S(2)}, u32[]{:S(2)}) collective-permute-start(bf16[256,2048]{1,0:T(8,128)(2,1)} %get-tuple-element.73), channel_id=1, source_target_pairs={{0,0},{4,4},{8,8},{12,28},{16,16},{20,20},{24,24},{28,44},{32,32},... | collective-permute-start | bytes 3145736 | tf_op jit(solution)/shard_map/cond/branch_3_fun/ppermute | solution.py:234
  124.9 31.1 %collective-permute-start.17 = (bf16[256,2048]{1,0:T(8,128)(2,1)S(1)}, bf16[256,2048]{1,0:T(8,128)(2,1)}, u32[]{:S(2)}, u32[]{:S(2)}) collective-permute-start(bf16[256,2048]{1,0:T(8,128)(2,1)S(1)} %collective-permute-done.16), channel_id=1, source_target_pairs={{0,16},{4,20},{8,8},{12,12},{16,32},{20,36},{24,24},{28,28},{32,48... | collective-permute-start | bytes 3145736 | tf_op jit(solution)/shard_map/cond/branch_3_fun/ppermute | solution.py:234
  128.2 41.8 %collective-permute-start.19 = (bf16[256,2048]{1,0:T(8,128)(2,1)S(1)}, bf16[256,2048]{1,0:T(8,128)(2,1)}, u32[]{:S(2)}, u32[]{:S(2)}) collective-permute-start(bf16[256,2048]{1,0:T(8,128)(2,1)S(1)} %collective-permute-done.18), channel_id=1, source_target_pairs={{0,8},{4,12},{8,0},{12,4},{16,24},{20,28},{24,16},{28,20},{32,40},... | collective-permute-start | bytes 3145736 | tf_op jit(solution)/shard_map/cond/branch_3_fun/ppermute | solution.py:229
  148.8 32.5 %collective-permute-start.21 = (bf16[256,2048]{1,0:T(8,128)(2,1)S(1)}, bf16[256,2048]{1,0:T(8,128)(2,1)}, u32[]{:S(2)}, u32[]{:S(2)}) collective-permute-start(bf16[256,2048]{1,0:T(8,128)(2,1)S(1)} %collective-permute-done.20), channel_id=1, source_target_pairs={{0,16},{4,4},{8,8},{12,12},{16,32},{20,20},{24,24},{28,28},{32,48}... | collective-permute-start | bytes 3145736 | tf_op jit(solution)/shard_map/cond/branch_3_fun/ppermute | solution.py:234
  152.0 41.1 %collective-permute-start.23 = (bf16[256,2048]{1,0:T(8,128)(2,1)S(1)}, bf16[256,2048]{1,0:T(8,128)(2,1)}, u32[]{:S(2)}, u32[]{:S(2)}) collective-permute-start(bf16[256,2048]{1,0:T(8,128)(2,1)S(1)} %collective-permute-done.22), channel_id=1, source_target_pairs={{0,4},{4,8},{8,12},{12,0},{16,20},{20,24},{24,28},{28,16},{32,36},... | collective-permute-start | bytes 3145736 | tf_op jit(solution)/shard_map/cond/branch_3_fun/ppermute | solution.py:229

commit v2 on v1

v2 whole, which is shorter than its diff:
```python
from functools import partial
import math

import jax
import jax.numpy as jnp
from jax import lax
from jax.experimental import pallas as pl
from jax.experimental.pallas import tpu as pltpu
from jax.sharding import PartitionSpec as P

EXPONENTS = 3
CHUNKS = 2
RING = 4
TILE = 1024
VMEM = 63 * 2**20

learning_rate = 0.5
epsilon = 1e-06


def swap(block, bit):
    n = lax.axis_size("fsdp")
    return lax.ppermute(block, "fsdp", [(i, i ^ bit) for i in range(n)])


def pushed(block, distance):
    n = lax.axis_size("gossip")
    return lax.ppermute(block, "gossip", [(i, (i + distance) % n) for i in range(n)])


def after(block, *earlier):
    return lax.optimization_barrier((block, *earlier))[0]


def norm(h):
    values = h.astype(jnp.float32)
    scale = lax.rsqrt(jnp.mean(values * values, axis=-1, keepdims=True) + epsilon)
    return (values * scale).astype(jnp.bfloat16)


def norm_kernel(h_ref, out_ref):
    out_ref[...] = norm(h_ref[0, 0])


def normalized(hidden_in, step):
    _, _, n_tok, width = hidden_in.shape
    tile = 128
    return pl.pallas_call(
        norm_kernel,
        grid=(n_tok // tile,),
        in_specs=[pl.BlockSpec((1, 1, tile, width), lambda i: (step, 0, i, 0))],
        out_specs=pl.BlockSpec((tile, width), lambda i: (i, 0)),
        out_shape=jax.ShapeDtypeStruct((n_tok, width), jnp.bfloat16),
        compiler_params=pltpu.CompilerParams(vmem_limit_bytes=VMEM),
        name="normalize",
    )(hidden_in)


def first_kernel(f_ref, h_ref, t0_ref, t1_ref, out_ref):
    step = pl.program_id(0)

    @pl.when(step == 0)
    def _():
        out_ref[...] = norm(h_ref[0, 0])

    @pl.when(step == 1)
    def _():
        half = out_ref.shape[1] // 2
        out_ref[:, :half] = t0_ref[0, 0]
        out_ref[:, half:] = t1_ref[0, 0]


def first_message(f, hidden_in, targets):
    _, _, n_tok, width = hidden_in.shape
    half = width // 2
    tile = 128
    per_step = n_tok // tile

    def of_step(step):
        return pl.BlockSpec(
            (1, 1, tile, half), lambda part, i, f: (step, 0, i * part, jnp.bitwise_xor(f[0] // 2, 1))
        )

    return pl.pallas_call(
        first_kernel,
        grid_spec=pltpu.PrefetchScalarGridSpec(
            num_scalar_prefetch=1,
            grid=(2, per_step),
            in_specs=[
                pl.BlockSpec((1, 1, tile, width), lambda part, i, f: (0, 0, i * (1 - part) + (per_step - 1) * part, 0)),
                of_step(0),
                of_step(1),
            ],
            out_specs=pl.BlockSpec((tile, width), lambda part, i, f: (part * per_step + i, 0)),
        ),
        out_shape=jax.ShapeDtypeStruct((2 * n_tok, width), jnp.bfloat16),
        compiler_params=pltpu.CompilerParams(vmem_limit_bytes=VMEM),
        name="first_message",
    )(f, hidden_in, targets, targets)


def copy_kernel(f_ref, t_ref, out_ref):
    out_ref[0] = t_ref[0, 0]


def for_other_core(f, targets, n_rows):
    steps, _, n_tok, _ = targets.shape
    return pl.pallas_call(
        copy_kernel,
        grid_spec=pltpu.PrefetchScalarGridSpec(
            num_scalar_prefetch=1,
            grid=(steps,),
            in_specs=[pl.BlockSpec((1, 1, n_tok, n_rows), lambda s, f: (s, 0, 0, jnp.bitwise_xor(f[0], 1)))],
            out_specs=pl.BlockSpec((1, n_tok, n_rows), lambda s, f: (s, 0, 0)),
        ),
        out_shape=jax.ShapeDtypeStruct((steps, n_tok, n_rows), jnp.bfloat16),
        compiler_params=pltpu.CompilerParams(vmem_limit_bytes=VMEM),
        name="pack_targets",
    )(f, targets)


def pair_kernel(last, w_ref, order_ref, f_ref, l0, l1, n0, n1, t0, t1, rows_ref, *refs, step):
    deltas = refs[-1]
    half, width = l0.shape
    root_width = math.sqrt(width)
    n_tok = n0.shape[0]

    @pl.when(pl.program_id(0) == 0)
    def _():
        scale = 2.0**step / (root_width * w_ref[0])
        for b, (n, t) in enumerate(((n0, t0), (n1, t1))):
            goals = t[...].reshape(t.shape[-2:])
            for c, left in enumerate((l0, l1)):
                pre = scale * lax.dot_general(
                    n[...], left[...], (((1,), (1,)), ((), ())), preferred_element_type=jnp.float32
                )
                goal = goals[:, c * half : (c + 1) * half].astype(jnp.float32)
                sigma = jax.nn.sigmoid(pre)
                slope = sigma * (1.0 + pre * (1.0 - sigma))
                delta = ((pre * sigma - goal) * slope).astype(jnp.bfloat16)
                deltas[c * half : (c + 1) * half, b * n_tok : (b + 1) * n_tok] = delta.T

    k = pl.ds(pl.multiple_of(pl.program_id(0) * TILE, TILE), TILE)
    total = jnp.dot(deltas[:, :n_tok], n0[:, k], preferred_element_type=jnp.float32)
    total += jnp.dot(deltas[:, n_tok:], n1[:, k], preferred_element_type=jnp.float32)
    rows = rows_ref[...] - (learning_rate / root_width) * total
    if not last:
        refs[0][...] = rows
        return
    halved = rows * 0.5
    refs[0][...] = halved
    for c, left in enumerate((l0, l1)):
        here = halved[c * half : (c + 1) * half]
        message = here.astype(jnp.bfloat16)
        if step == 0:
            refs[1 + c][...] = message
        else:
            earlier = left[:, k]
            both = (earlier.astype(jnp.float32) + here).astype(jnp.bfloat16)
            swapped = order_ref[0] > order_ref[1]
            near = jnp.where(swapped, message, earlier)
            refs[1 + c][...] = jnp.where(order_ref[0] == order_ref[1], both, near)
            refs[3 + c][...] = jnp.where(swapped, earlier, message)


def pair(step, last, weight, order, f, n_tok, left, ns, ts, rows):
    n_rows, width = rows.shape
    half = n_rows // CHUNKS

    def goal(t):
        if t.ndim == 4:
            return pl.BlockSpec((1, 1, n_tok, n_rows), lambda j, w, s, f: (step, 0, 0, f[0]))
        if t.ndim == 3:
            return pl.BlockSpec((1, n_tok, n_rows), lambda j, w, s, f: (step, 0, 0))
        return pl.BlockSpec((n_tok, n_rows), lambda j, w, s, f: (1, step * 2 + f[0] % 2))

    if len(left) == 1:
        left = [left[0], left[0]]
        halves = [pl.BlockSpec((half, width), lambda j, w, s, f, c=c: (c, 0)) for c in range(CHUNKS)]
    else:
        halves = [pl.BlockSpec((half, width), lambda j, w, s, f: (0, 0))] * CHUNKS
    tile = pl.BlockSpec((n_rows, TILE), lambda j, w, s, f: (0, j))
    out_specs = [tile]
    out_shape = [jax.ShapeDtypeStruct((n_rows, width), jnp.float32)]
    if last:
        out_specs += [pl.BlockSpec((half, TILE), lambda j, w, s, f: (0, j))] * (2 + 2 * step)
        out_shape += [jax.ShapeDtypeStruct((half, width), jnp.bfloat16)] * (2 + 2 * step)
    return pl.pallas_call(
        partial(pair_kernel, last, step=step),
        grid_spec=pltpu.PrefetchScalarGridSpec(
            num_scalar_prefetch=3,
            grid=(width // TILE,),
            in_specs=halves
            + [pl.BlockSpec((n_tok, width), lambda j, w, s, f: (0, 0))] * 2
            + [goal(t) for t in ts]
            + [tile],
            out_specs=out_specs,
            scratch_shapes=[pltpu.VMEM((n_rows, 2 * n_tok), jnp.bfloat16)],
        ),
        out_shape=out_shape,
        compiler_params=pltpu.CompilerParams(vmem_limit_bytes=VMEM),
        cost_estimate=pl.CostEstimate(flops=2**20, bytes_accessed=2**20, transcendentals=0),
        name="pair_of_blocks",
    )(weight, order, f, *left, *ns, *ts, rows)


def sum_kernel(chunks, n_arrived, w_ref, *refs):
    source, arrived = refs[0], refs[1 : 1 + len(chunks) * n_arrived]
    out = refs[-(n_arrived + 4)]
    bufs, (in_sems, out_sems) = refs[-(n_arrived + 3) : -2], refs[-2:]
    pieces = in_sems.shape[2]
    count = bufs[0].shape[0] // len(chunks)
    piece = count // pieces
    factor = 1.0 / w_ref[0]

    def rows(at, i):
        return pl.ds(pl.multiple_of(at * count + i * piece, piece), piece)

    def copies_in(c, i):
        froms = [source.at[rows(chunks[c], i)]]
        froms += [a.at[rows(0, i)] for a in arrived[c * n_arrived : (c + 1) * n_arrived]]
        return [
            pltpu.make_async_copy(x, bufs[a].at[rows(c, i)], in_sems.at[c, a, i]) for a, x in enumerate(froms)
        ]

    def copy_out(c, i):
        return pltpu.make_async_copy(bufs[0].at[rows(c, i)], out.at[rows(chunks[c], i)], out_sems.at[c, i])

    def run(c, body):
        lax.fori_loop(0, pieces, lambda i, _: (body(c, i), 0)[1], 0)

    def start(c, i):
        for x in copies_in(c, i):
            x.start()

    def work(c, i):
        for x in copies_in(c, i):
            x.wait()

        def strip(j, _):
            s = pl.ds(pl.multiple_of(c * count + i * piece + j * 16, 16), 16)
            total = bufs[0][s]
            for a in bufs[1:]:
                total = total + a[s].astype(jnp.float32)
            bufs[0][s] = total * factor
            return 0

        lax.fori_loop(0, piece // 16, strip, 0)
        copy_out(c, i).start()

    for body in (start, work, lambda c, i: copy_out(c, i).wait()):
        for c in range(len(chunks)):
            run(c, body)


def divided(weight, halved, chunks, arrived, out=None):
    n_rows, width = halved.shape
    count = n_rows // CHUNKS
    pieces = 4
    n_arrived = len(arrived[0])
    operands = [halved] + [x for messages in arrived for x in messages]
    aliases = {}
    if out is not None:
        operands.append(out)
        aliases = {len(operands): 0}
    anywhere = pl.BlockSpec(memory_space=pl.ANY)
    return pl.pallas_call(
        partial(sum_kernel, chunks, n_arrived),
        grid_spec=pltpu.PrefetchScalarGridSpec(
            num_scalar_prefetch=1,
            grid=(),
            in_specs=[anywhere] * len(operands),
            out_specs=anywhere,
            scratch_shapes=[pltpu.VMEM((len(chunks) * count, width), jnp.float32)]
            + [pltpu.VMEM((len(chunks) * count, width), jnp.bfloat16)] * n_arrived
            + [
                pltpu.SemaphoreType.DMA((len(chunks), 1 + n_arrived, pieces)),
                pltpu.SemaphoreType.DMA((len(chunks), pieces)),
            ],
        ),
        out_shape=jax.ShapeDtypeStruct((n_rows, width), jnp.float32),
        input_output_aliases=aliases,
        compiler_params=pltpu.CompilerParams(vmem_limit_bytes=VMEM),
        name="last_sum",
    )(weight, *operands)


def along(block, distance):
    n = lax.axis_size("gossip")
    return lax.ppermute(block, "gossip", [(i, i - i % RING + (i + distance) % RING) for i in range(n)])


def across(block, wrapped):
    n = lax.axis_size("gossip")
    return lax.ppermute(block, "gossip", [(i, (i + RING) % n if i % RING in wrapped else i) for i in range(n)])


def back_across(block, distance):
    n = lax.axis_size("gossip")
    to = [i - i % RING + (i - 1) % RING for i in range(n)]
    return lax.ppermute(block, "gossip", [(i, (t + RING) % n if t % RING < distance else t) for i, t in enumerate(to)])


def finish(near, far, weight, halved, m_near, m_far):
    if near == far:
        arrived = [pushed(m, 1 << near) for m in m_near]
        out = divided(weight, halved, (0,), [arrived[:1]])
        return divided(weight, halved, (1,), [arrived[1:]], out)
    first, second = exchange(near, far, m_near, m_far)
    return divided(weight, halved, (0, 1), list(zip(first, second)))


def exchange(k0, k1, m0, m1):
    crowded = max(1 << k0, 1 << k1) < RING
    begun = []
    for k, m in ((k0, m0), (k1, m1)):
        d = 1 << k
        if d >= RING:
            begun.append([pushed(x, d) for x in m])
        elif crowded and 2 * d == RING:
            begun.append([along(m[0], -1), m[1]])
        else:
            begun.append([along(m[0], d), across(m[1], range(RING - d, RING))])
    sent = []
    for k, m in zip((k0, k1), begun):
        d = 1 << k
        if d >= RING:
            sent.append(m)
        elif crowded and 2 * d == RING:
            sent.append([back_across(m[0], d), pushed(after(m[1], begun[0][0]), d)])
        else:
            sent.append([across(m[0], range(d)), along(m[1], d)])
    return sent[0], sent[1]


def per_device(numerator, push_weight, hidden_in, targets, exponents):
    numerators = numerator[0]
    n_rows, width = numerators.shape
    weight = push_weight.astype(jnp.float32)
    order = exponents
    f = lax.axis_index("fsdp").astype(jnp.int32)[None]

    n_tok = hidden_in.shape[2]
    mine0 = first_message(f, hidden_in, targets)
    chip0 = swap(mine0, 2)
    own0 = lax.slice(mine0, (0, 0), (n_tok, width))
    core0 = swap(own0, 1)
    t_core = swap(for_other_core(after(f, mine0), targets, n_rows), 1)
    own1 = normalized(after(hidden_in, mine0), 1)
    chip1 = swap(own1, 2)
    core1 = swap(own1, 1)
    current0 = after(numerators, own1).astype(jnp.bfloat16)
    step = partial(pair, weight=weight, order=order, f=f, n_tok=n_tok)
    [rows0] = step(0, False, left=[current0], ns=[own0, core0], ts=[targets, t_core], rows=numerators)

    received = []
    tile = after(jnp.broadcast_to(push_weight, (16, 128)), rows0)
    for k in range(EXPONENTS):
        tile = after(tile, *received)
        received.append(pushed(tile, 1 << k))
    received = [x[0, :1].astype(jnp.float32) for x in received]

    def chosen(k):
        return jnp.where(k == 0, received[0], jnp.where(k == 1, received[1], received[2]))

    weight_out = (weight * 0.25 + chosen(order[0]) * 0.5) + chosen(order[1]) * 0.25

    chip0 = after(chip0, weight_out)
    far0 = [chip0, swap(chip0, 1)]
    halved0, *m0 = step(0, True, left=[current0], ns=far0, ts=far0, rows=rows0)
    [rows1] = step(1, False, left=m0, ns=[own1, core1], ts=[targets, t_core], rows=halved0)
    chip1 = after(chip1, rows1)
    halved1, a0, a1, b0, b1 = step(1, True, left=m0, ns=[chip1, swap(chip1, 1)], ts=far0, rows=rows1)

    cases = [(near, far) for far in range(EXPONENTS) for near in range(far + 1)]
    near, far = jnp.minimum(order[0], order[1]), jnp.maximum(order[0], order[1])
    params = lax.switch(
        far * (far + 1) // 2 + near, [partial(finish, *c) for c in cases], weight_out, halved1, [a0, a1], [b0, b1]
    )
    return params[None], weight_out


def solution(mesh):
    in_specs = (
        P("gossip", "fsdp", None),
        P("gossip"),
        P(None, "gossip", "fsdp", None),
        P(None, "gossip", "fsdp", None),
        P(),
    )
    out_specs = (P("gossip", "fsdp", None), P("gossip"))
    return jax.shard_map(
        per_device, mesh=mesh, in_specs=in_specs, out_specs=out_specs, check_vma=False
    )
```

time: 210 us -> 183 us (0.87)
  starting transfers between devices: 31.3 us -> 13.3 us
  loops' own time: 8.69 us -> 0.29 us
  waiting for transfers between devices: 95.2 us -> 99.8 us
  Pallas kernels: 50.8 us -> 48.3 us
    ppermute x4 -> x2, waiting for transfers between devices: 59.7 us -> 23.9 us  [along(): lax.ppermute(block, 'gossip', [(i, i - i % RING + (i + distance) % RING)...]
    ppermute x3 -> x5, waiting for transfers between devices: 18.9 us -> 45.3 us  [pushed(): lax.ppermute(block, 'gossip', [(i, (i + distance) % n) for i in range(n)])]
    ppermute x4 -> x2, starting transfers between devices: 9.17 us -> 0.17 us  [along(): lax.ppermute(block, 'gossip', [(i, i - i % RING + (i + distance) % RING)...]
    another operation x1, loops' own time: 8.69 us -> 0.29 us  [per_device(): lax.switch(far * (far + 1) // 2 + near, [partial(finish, *c) for c in cas...]
    ppermute x4 -> x2, waiting for transfers between devices: 15.3 us -> 22.5 us  [across(): lax.ppermute(block, 'gossip', [(i, (i + RING) % n if i % RING in wrapped...]
    ppermute x9 -> x7, waiting for transfers between devices: 1.34 us -> 8.05 us  [swap(): return lax.ppermute(block, 'fsdp', [(i, i ^ bit) for i in range(n)])]
    ppermute x4 -> x2, starting transfers between devices: 10.2 us -> 3.79 us  [across(): lax.ppermute(block, 'gossip', [(i, (i + RING) % n if i % RING in wrapped...]
    unnamed x13 -> x4, local copies, waits for them, and re-layouts: 3.48 us -> 0.8 us
  transfers between devices with their start and end apart: 20 -> 16, of which waited for: 9 -> 10; matrix products, arithmetic and copies ran while one was open for 5% -> 5% of each run, Pallas kernels for 16% -> 16%
where the time goes in v2:
time: 183 us; the launch traced here: 182 us
  waiting for transfers between devices  99.8 us (55%)
  Pallas kernels  48.3 us (26%)
  starting transfers between devices  13.3 us (7%)
  between operations  11.2 us (6%)
  local copies, waits for them, and re-layouts  5.4 us (3%)
  other arithmetic  3.86 us (2%)
    ppermute x5, waiting for transfers between devices, pushed(): lax.ppermute(block, 'gossip', [(i, (i + distance) % n) for i in range(n)])  45.3 us
    pallas_call x4, Pallas kernels, pair(): pl.pallas_call(partial(pair_kernel, last, step=step), grid_spec=pltpu.Pre...  34.4 us
    ppermute x2, waiting for transfers between devices, along(): lax.ppermute(block, 'gossip', [(i, i - i % RING + (i + distance) % RING)...  23.9 us
    ppermute x2, waiting for transfers between devices, across(): lax.ppermute(block, 'gossip', [(i, (i + RING) % n if i % RING in wrapped...  22.5 us
    ppermute x7, starting transfers between devices, swap(): return lax.ppermute(block, 'fsdp', [(i, i ^ bit) for i in range(n)])  8.26 us
    ppermute x7, waiting for transfers between devices, swap(): return lax.ppermute(block, 'fsdp', [(i, i ^ bit) for i in range(n)])  8.05 us
    pallas_call x1, Pallas kernels, divided(): pl.pallas_call(partial(sum_kernel, chunks, n_arrived), grid_spec=pltpu.Pr...  5.53 us
    pallas_call x1, Pallas kernels, first_message(): pl.pallas_call(first_kernel, grid_spec=pltpu.PrefetchScalarGridSpec(num_s...  4.32 us
  transfers between devices with their start and end apart: 16, of which 10 were waited for; matrix products, arithmetic and copies ran while one was open for 5% of the time, Pallas kernels for 16%

profile of v2, /device:TPU:1, one launch (start us, length us, event | category | flops | bytes accessed | tf_op | source)
XLA Modules:
  0.0 182.1 jit_solution(475681081841363239)
XLA Ops:
  0.6 4.3 %first_message.1 = bf16[512,2048]{1,0:T(8,128)(2,1)} custom-call(s32[1]{0:T(128)} %bitcast.8.f_ref, bf16[2,1,256,2048]{3,2,1,0:T(8,128)(2,1)} %h_ref.2, bf16[2,1,256,2048]{3,2,1,0:T(8,128)(2,1)} %t0.3, bf16[2,1,256,2048]{3,2,1,0:T(8,128)(2,1)} %t0.3), custom_call_target="tpu_custom_call" | custom-call | tf_op jit(solution)/shard_map/first_message/pallas_call | solution.py:84
  5.0 2.1 %collective-permute-start.25 = (bf16[512,2048]{1,0:T(8,128)(2,1)}, bf16[512,2048]{1,0:T(8,128)(2,1)}, u32[]{:S(2)}, u32[]{:S(2)}) collective-permute-start(bf16[512,2048]{1,0:T(8,128)(2,1)} %first_message.1), channel_id=1, source_target_pairs={{0,2},{1,3},{2,0},{3,1},{4,6},{5,7},{6,4},{7,5},{8,10},{9,11},{10,... | collective-permute-start | bytes 6291464 | tf_op jit(solution)/shard_map/ppermute | solution.py:23
  7.1 2.4 %slice.28.n0 = bf16[256,2048]{1,0:T(8,128)(2,1)} slice(bf16[512,2048]{1,0:T(8,128)(2,1)} %first_message.1), slice={[0:256], [0:2048]} | slice | bytes 2097152 | tf_op jit(solution)/shard_map/slice | solution.py:346
  9.4 1.1 collective-permute-start.26
  10.6 1.8 pack_targets.1
  12.3 0.0 collective-permute-start.27
  13.0 2.2 %normalize.1.n0 = bf16[256,2048]{1,0:T(8,128)(2,1)} custom-call(bf16[2,1,256,2048]{3,2,1,0:T(8,128)(2,1)} %h_ref.2), custom_call_target="tpu_custom_call" | custom-call | tf_op jit(solution)/shard_map/normalize/pallas_call | solution.py:48
  15.2 3.9 %convert_element_type.25.l0.l1 = bf16[512,2048]{1,0:T(8,128)(2,1)} convert(f32[512,2048]{1,0:T(8,128)} %bitcast.24) | non-fusion elementwise | flops 1048576 | bytes 6291456 | tf_op jit(solution)/shard_map/convert_element_type | solution.py:352
  19.1 0.0 copy-start.1
  19.1 0.0 collective-permute-done.27.t1
  19.1 0.0 copy-start
  19.1 0.0 collective-permute-done.26.n1
  19.1 0.8 copy-done
  19.9 8.0 %pair_of_blocks.4.rows_ref = f32[512,2048]{1,0:T(8,128)} custom-call(f32[1]{0:T(128)S(6)} %convert_element_type.24.w_ref, s32[2]{0:T(128)} %order_ref.7, s32[1]{0:T(128)} %bitcast.8.f_ref, bf16[512,2048]{1,0:T(8,128)(2,1)} %convert_element_type.25.l0.l1, bf16[512,2048]{1,0:T(8,128)(2,1)} %convert_element_type.25.l0.l1, bf16[256,2048]{1,0:T(8,128)(2,1)} %slice.28.n0, ...), custom_call_target="tpu_custom_call" | custom-call | flops 1048576 | bytes 1048576 | tf_op jit(solution)/shard_map/pair_of_blocks/pallas_call | solution.py:188
  28.0 1.0 collective-permute-start.28
  29.0 10.0 %collective-permute-done.28 = bf16[16,128]{1,0:T(8,128)(2,1)S(1)} collective-permute-done((bf16[16,128]{1,0:T(8,128)(2,1)S(1)}, bf16[16,128]{1,0:T(8,128)(2,1)S(1)}, u32[]{:S(2)}, u32[]{:S(2)}) %collective-permute-start.28) | collective-permute-done | bytes 4128 | tf_op jit(solution)/shard_map/ppermute | solution.py:28
  39.0 0.0 collective-permute-start.29
  39.0 8.6 %collective-permute-done.29 = bf16[16,128]{1,0:T(8,128)(2,1)S(1)} collective-permute-done((bf16[16,128]{1,0:T(8,128)(2,1)S(1)}, bf16[16,128]{1,0:T(8,128)(2,1)S(1)}, u32[]{:S(2)}, u32[]{:S(2)}) %collective-permute-start.29) | collective-permute-done | bytes 4128 | tf_op jit(solution)/shard_map/ppermute | solution.py:28
  47.6 0.0 collective-permute-start.30
  47.6 0.0 copy-done.1
  47.6 0.6 fusion
  50.7 0.5 slice.29
  51.2 0.6 slice.30
  51.7 2.0 %collective-permute-done.30 = bf16[16,128]{1,0:T(8,128)(2,1)S(1)} collective-permute-done((bf16[16,128]{1,0:T(8,128)(2,1)S(1)}, bf16[16,128]{1,0:T(8,128)(2,1)S(1)}, u32[]{:S(2)}, u32[]{:S(2)}) %collective-permute-start.30) | collective-permute-done | bytes 4128 | tf_op jit(solution)/shard_map/ppermute | solution.py:28
  53.8 0.5 slice.31
  58.1 0.0 collective-permute-done.25.n0.t0
  58.1 3.7 %collective-permute-start.31 = (bf16[512,2048]{1,0:T(8,128)(2,1)}, bf16[512,2048]{1,0:T(8,128)(2,1)}, u32[]{:S(2)}, u32[]{:S(2)}) collective-permute-start(bf16[512,2048]{1,0:T(8,128)(2,1)} %collective-permute-done.25.n0.t0), channel_id=1, source_target_pairs={{0,1},{1,0},{2,3},{3,2},{4,5},{5,4},{6,7},{7,6},{8,9},{9,8},{10,11... | collective-permute-start | bytes 6291464 | tf_op jit(solution)/shard_map/ppermute | solution.py:23
  61.8 0.1 collective-permute-start.33
  61.9 0.0 collective-permute-start.32
  61.9 4.0 %collective-permute-done.31.n1.t1 = bf16[512,2048]{1,0:T(8,128)(2,1)} collective-permute-done((bf16[512,2048]{1,0:T(8,128)(2,1)}, bf16[512,2048]{1,0:T(8,128)(2,1)}, u32[]{:S(2)}, u32[]{:S(2)}) %collective-permute-start.31) | collective-permute-done | bytes 2097184 | tf_op jit(solution)/shard_map/ppermute | solution.py:23
  65.9 8.7 %pair_of_blocks.5 = (f32[512,2048]{1,0:T(8,128)}, bf16[256,2048]{1,0:T(8,128)(2,1)}, bf16[256,2048]{1,0:T(8,128)(2,1)}) custom-call(f32[1]{0:T(128)S(6)} %convert_element_type.24.w_ref, s32[2]{0:T(128)} %order_ref.7, s32[1]{0:T(128)} %bitcast.8.f_ref, bf16[512,2048]{1,0:T(8,128)(2,1)} %convert_element_type.25.l0.l1, ...), custom_call_target="tpu_custom_call" | custom-call | flops 1048576 | bytes 1048576 | tf_op jit(solution)/shard_map/pair_of_blocks/pallas_call | solution.py:188
  74.6 0.0 collective-permute-done.33.n1
  74.6 8.1 %pair_of_blocks.6.rows_ref = f32[512,2048]{1,0:T(8,128)} custom-call(f32[1]{0:T(128)S(6)} %convert_element_type.24.w_ref, s32[2]{0:T(128)} %order_ref.7, s32[1]{0:T(128)} %bitcast.8.f_ref, bf16[256,2048]{1,0:T(8,128)(2,1)} %get-tuple-element.124.l0, bf16[256,2048]{1,0:T(8,128)(2,1)} %get-tuple-element.125.l1, bf16[256,2048]{1,0:T(8,128)(2,1)} %normalize.1.n0, ...), custom_call_target="tpu_custom_call" | custom-call | flops 1048576 | bytes 1048576 | tf_op jit(solution)/shard_map/pair_of_blocks/pallas_call | solution.py:188
  82.7 3.8 %collective-permute-done.32.n0 = bf16[256,2048]{1,0:T(8,128)(2,1)} collective-permute-done((bf16[256,2048]{1,0:T(8,128)(2,1)}, bf16[256,2048]{1,0:T(8,128)(2,1)}, u32[]{:S(2)}, u32[]{:S(2)}) %collective-permute-start.32) | collective-permute-done | bytes 1048608 | tf_op jit(solution)/shard_map/ppermute | solution.py:23
  86.5 1.2 collective-permute-start.34
  90.3 0.2 collective-permute-done.34.n1
  90.4 9.6 %pair_of_blocks.7 = (f32[512,2048]{1,0:T(8,128)}, bf16[256,2048]{1,0:T(8,128)(2,1)}, bf16[256,2048]{1,0:T(8,128)(2,1)}, bf16[256,2048]{1,0:T(8,128)(2,1)}, bf16[256,2048]{1,0:T(8,128)(2,1)}) custom-call(f32[1]{0:T(128)S(6)} %convert_element_type.24.w_ref, s32[2]{0:T(128)} %order_ref.7, s32[1]{0:T(128)} %bitcast.8.f_ref, ...), custom_call_target="tpu_custom_call" | custom-call | flops 1048576 | bytes 1048576 | tf_op jit(solution)/shard_map/pair_of_blocks/pallas_call | solution.py:188
  100.0 80.9 %conditional.1 = (f32[1,512,2048]{2,1,0:T(8,128)}) conditional(s32[]{:T(128)} %clamp.3, (bf16[256,2048]{1,0:T(8,128)(2,1)}, bf16[256,2048]{1,0:T(8,128)(2,1)}, f32[1]{0:T(128)}, f32[512,2048]{1,0:T(8,128)}) %tuple.49, (bf16[256,2048]{1,0:T(8,128)(2,1)}, bf16[256,2048]{1,0:T(8,128)(2,1)}, bf16[256,2048]{1,0:T(8,128)(2,1)}, ...), branch_computations={%region_0.1_spmd, %region_1.2_spmd, %region_2.3_spmd, %region_3.4_... | conditional | bytes 29360416 | solution.py:377
  100.2 0.1 collective-permute-start.11
  100.3 1.9 %collective-permute-start.14 = (bf16[256,2048]{1,0:T(8,128)(2,1)}, bf16[256,2048]{1,0:T(8,128)(2,1)S(1)}, u32[]{:S(2)}, u32[]{:S(2)}) collective-permute-start(bf16[256,2048]{1,0:T(8,128)(2,1)} %get-tuple-element.87), channel_id=1, source_target_pairs={{0,0},{4,4},{8,8},{12,28},{16,16},{20,20},{24,24},{28,44},{32,32},... | collective-permute-start | bytes 3145736 | tf_op jit(solution)/shard_map/cond/branch_3_fun/ppermute | solution.py:295
  102.2 0.0 collective-permute-start.13
  102.2 0.0 collective-permute-start.16
  102.2 23.9 %collective-permute-done.11 = bf16[256,2048]{1,0:T(8,128)(2,1)S(1)} collective-permute-done((bf16[256,2048]{1,0:T(8,128)(2,1)}, bf16[256,2048]{1,0:T(8,128)(2,1)S(1)}, u32[]{:S(2)}, u32[]{:S(2)}) %collective-permute-start.11) | collective-permute-done | bytes 1048608 | tf_op jit(solution)/shard_map/cond/branch_3_fun/ppermute | solution.py:290
  126.1 1.9 %collective-permute-start.12 = (bf16[256,2048]{1,0:T(8,128)(2,1)S(1)}, bf16[256,2048]{1,0:T(8,128)(2,1)}, u32[]{:S(2)}, u32[]{:S(2)}) collective-permute-start(bf16[256,2048]{1,0:T(8,128)(2,1)S(1)} %collective-permute-done.11), channel_id=1, source_target_pairs={{0,16},{4,4},{8,8},{12,12},{16,32},{20,20},{24,24},{28,28},{32,48}... | collective-permute-start | bytes 3145736 | tf_op jit(solution)/shard_map/cond/branch_3_fun/ppermute | solution.py:295
  128.1 0.0 collective-permute-done.14
  128.1 0.1 collective-permute-start.15
  128.2 2.3 %collective-permute-done.13.refs_2_ = bf16[256,2048]{1,0:T(8,128)(2,1)} collective-permute-done((bf16[256,2048]{1,0:T(8,128)(2,1)}, bf16[256,2048]{1,0:T(8,128)(2,1)}, u32[]{:S(2)}, u32[]{:S(2)}) %collective-permute-start.13) | collective-permute-done | bytes 1048608 | tf_op jit(solution)/shard_map/cond/branch_3_fun/ppermute | solution.py:28
  130.4 22.5 %collective-permute-done.16.refs_4_ = bf16[256,2048]{1,0:T(8,128)(2,1)} collective-permute-done((bf16[256,2048]{1,0:T(8,128)(2,1)}, bf16[256,2048]{1,0:T(8,128)(2,1)}, u32[]{:S(2)}, u32[]{:S(2)}) %collective-permute-start.16) | collective-permute-done | bytes 1048608 | tf_op jit(solution)/shard_map/cond/branch_3_fun/ppermute | solution.py:28
  152.9 22.5 %collective-permute-done.12.refs_1_ = bf16[256,2048]{1,0:T(8,128)(2,1)} collective-permute-done((bf16[256,2048]{1,0:T(8,128)(2,1)S(1)}, bf16[256,2048]{1,0:T(8,128)(2,1)}, u32[]{:S(2)}, u32[]{:S(2)}) %collective-permute-start.12) | collective-permute-done | bytes 1048608 | tf_op jit(solution)/shard_map/cond/branch_3_fun/ppermute | solution.py:295
  175.4 0.0 collective-permute-done.15.refs_3_
  175.4 5.5 %last_sum.14 = f32[512,2048]{1,0:T(8,128)} custom-call(f32[1]{0:T(128)} %get-tuple-element.83.w_ref, f32[512,2048]{1,0:T(8,128)} %get-tuple-element.84.refs_0_, bf16[256,2048]{1,0:T(8,128)(2,1)} %collective-permute-done.12.refs_1_, bf16[256,2048]{1,0:T(8,128)(2,1)} %collective-permute-done.13.refs_2_, bf16[256,2048]{1,0:T(8,128)(2,1)} %collective-permute-done.15.refs_3_, ...), custom_call_target="tpu_custom_call" | custom-call | tf_op jit(solution)/shard_map/cond/branch_3_fun/last_sum/pallas_call | solution.py:267
  (1 shorter events, 0.0 us)
Async XLA Ops:
  5.0 53.2 %collective-permute-start.25 = (bf16[512,2048]{1,0:T(8,128)(2,1)}, bf16[512,2048]{1,0:T(8,128)(2,1)}, u32[]{:S(2)}, u32[]{:S(2)}) collective-permute-start(bf16[512,2048]{1,0:T(8,128)(2,1)} %first_message.1), channel_id=1, source_target_pairs={{0,2},{1,3},{2,0},{3,1},{4,6},{5,7},{6,4},{7,5},{8,10},{9,11},{10,... | collective-permute-start | bytes 6291464 | tf_op jit(solution)/shard_map/ppermute | solution.py:23
  9.4 9.7 %collective-permute-start.26 = (bf16[256,2048]{1,0:T(8,128)(2,1)}, bf16[256,2048]{1,0:T(8,128)(2,1)}, u32[]{:S(2)}, u32[]{:S(2)}) collective-permute-start(bf16[256,2048]{1,0:T(8,128)(2,1)} %slice.28.n0), channel_id=1, source_target_pairs={{0,1},{1,0},{2,3},{3,2},{4,5},{5,4},{6,7},{7,6},{8,9},{9,8},{10,11... | collective-permute-start | bytes 3145736 | tf_op jit(solution)/shard_map/ppermute | solution.py:23
  12.3 6.8 %collective-permute-start.27 = (bf16[2,256,512]{2,1,0:T(8,128)(2,1)}, bf16[2,256,512]{2,1,0:T(8,128)(2,1)S(1)}, u32[]{:S(2)}, u32[]{:S(2)}) collective-permute-start(bf16[2,256,512]{2,1,0:T(8,128)(2,1)} %pack_targets.1), channel_id=1, source_target_pairs={{0,1},{1,0},{2,3},{3,2},{4,5},{5,4},{6,7},{7,6},{8,9},{9,8},{10,11... | collective-permute-start | bytes 1572872 | tf_op jit(solution)/shard_map/ppermute | solution.py:23
  19.1 28.5 %copy-start.1 = (s32[2]{0:T(128)S(1)}, s32[2]{0:T(128)}, u32[]{:S(2)}) copy-start(s32[2]{0:T(128)} %order_ref.7) | copy-start | bytes 28
  19.1 0.8 copy-start
  28.0 11.0 %collective-permute-start.28 = (bf16[16,128]{1,0:T(8,128)(2,1)S(1)}, bf16[16,128]{1,0:T(8,128)(2,1)S(1)}, u32[]{:S(2)}, u32[]{:S(2)}) collective-permute-start(bf16[16,128]{1,0:T(8,128)(2,1)S(1)} %broadcast_in_dim.28), channel_id=1, source_target_pairs={{0,4},{4,8},{8,12},{12,16},{16,20},{20,24},{24,28},{28,32},{32,36}... | collective-permute-start | bytes 12296 | tf_op jit(solution)/shard_map/ppermute | solution.py:28
  39.0 8.6 %collective-permute-start.29 = (bf16[16,128]{1,0:T(8,128)(2,1)S(1)}, bf16[16,128]{1,0:T(8,128)(2,1)S(1)}, u32[]{:S(2)}, u32[]{:S(2)}) collective-permute-start(bf16[16,128]{1,0:T(8,128)(2,1)S(1)} %broadcast_in_dim.28), channel_id=1, source_target_pairs={{0,8},{4,12},{8,16},{12,20},{16,24},{20,28},{24,32},{28,36},{32,40... | collective-permute-start | bytes 12296 | tf_op jit(solution)/shard_map/ppermute | solution.py:28
  47.6 6.2 %collective-permute-start.30 = (bf16[16,128]{1,0:T(8,128)(2,1)S(1)}, bf16[16,128]{1,0:T(8,128)(2,1)S(1)}, u32[]{:S(2)}, u32[]{:S(2)}) collective-permute-start(bf16[16,128]{1,0:T(8,128)(2,1)S(1)} %broadcast_in_dim.28), channel_id=1, source_target_pairs={{0,16},{4,20},{8,24},{12,28},{16,32},{20,36},{24,40},{28,44},{32,4... | collective-permute-start | bytes 12296 | tf_op jit(solution)/shard_map/ppermute | solution.py:28
  58.1 7.8 %collective-permute-start.31 = (bf16[512,2048]{1,0:T(8,128)(2,1)}, bf16[512,2048]{1,0:T(8,128)(2,1)}, u32[]{:S(2)}, u32[]{:S(2)}) collective-permute-start(bf16[512,2048]{1,0:T(8,128)(2,1)} %collective-permute-done.25.n0.t0), channel_id=1, source_target_pairs={{0,1},{1,0},{2,3},{3,2},{4,5},{5,4},{6,7},{7,6},{8,9},{9,8},{10,11... | collective-permute-start | bytes 6291464 | tf_op jit(solution)/shard_map/ppermute | solution.py:23
  61.8 12.8 %collective-permute-start.33 = (bf16[256,2048]{1,0:T(8,128)(2,1)}, bf16[256,2048]{1,0:T(8,128)(2,1)}, u32[]{:S(2)}, u32[]{:S(2)}) collective-permute-start(bf16[256,2048]{1,0:T(8,128)(2,1)} %normalize.1.n0), channel_id=1, source_target_pairs={{0,1},{1,0},{2,3},{3,2},{4,5},{5,4},{6,7},{7,6},{8,9},{9,8},{10,11... | collective-permute-start | bytes 3145736 | tf_op jit(solution)/shard_map/ppermute | solution.py:23
  61.9 24.6 %collective-permute-start.32 = (bf16[256,2048]{1,0:T(8,128)(2,1)}, bf16[256,2048]{1,0:T(8,128)(2,1)}, u32[]{:S(2)}, u32[]{:S(2)}) collective-permute-start(bf16[256,2048]{1,0:T(8,128)(2,1)} %normalize.1.n0), channel_id=1, source_target_pairs={{0,2},{1,3},{2,0},{3,1},{4,6},{5,7},{6,4},{7,5},{8,10},{9,11},{10,... | collective-permute-start | bytes 3145736 | tf_op jit(solution)/shard_map/ppermute | solution.py:23
  86.5 3.9 %collective-permute-start.34 = (bf16[256,2048]{1,0:T(8,128)(2,1)}, bf16[256,2048]{1,0:T(8,128)(2,1)}, u32[]{:S(2)}, u32[]{:S(2)}) collective-permute-start(bf16[256,2048]{1,0:T(8,128)(2,1)} %collective-permute-done.32.n0), channel_id=1, source_target_pairs={{0,1},{1,0},{2,3},{3,2},{4,5},{5,4},{6,7},{7,6},{8,9},{9,8},{10,11... | collective-permute-start | bytes 3145736 | tf_op jit(solution)/shard_map/ppermute | solution.py:23
  100.2 25.9 %collective-permute-start.11 = (bf16[256,2048]{1,0:T(8,128)(2,1)}, bf16[256,2048]{1,0:T(8,128)(2,1)S(1)}, u32[]{:S(2)}, u32[]{:S(2)}) collective-permute-start(bf16[256,2048]{1,0:T(8,128)(2,1)} %get-tuple-element.85), channel_id=1, source_target_pairs={{0,4},{4,8},{8,12},{12,0},{16,20},{20,24},{24,28},{28,16},{32,36},... | collective-permute-start | bytes 3145736 | tf_op jit(solution)/shard_map/cond/branch_3_fun/ppermute | solution.py:290
  100.3 27.7 %collective-permute-start.14 = (bf16[256,2048]{1,0:T(8,128)(2,1)}, bf16[256,2048]{1,0:T(8,128)(2,1)S(1)}, u32[]{:S(2)}, u32[]{:S(2)}) collective-permute-start(bf16[256,2048]{1,0:T(8,128)(2,1)} %get-tuple-element.87), channel_id=1, source_target_pairs={{0,0},{4,4},{8,8},{12,28},{16,16},{20,20},{24,24},{28,44},{32,32},... | collective-permute-start | bytes 3145736 | tf_op jit(solution)/shard_map/cond/branch_3_fun/ppermute | solution.py:295
  102.2 28.2 %collective-permute-start.13 = (bf16[256,2048]{1,0:T(8,128)(2,1)}, bf16[256,2048]{1,0:T(8,128)(2,1)}, u32[]{:S(2)}, u32[]{:S(2)}) collective-permute-start(bf16[256,2048]{1,0:T(8,128)(2,1)} %get-tuple-element.86), channel_id=1, source_target_pairs={{0,16},{4,20},{8,24},{12,28},{16,32},{20,36},{24,40},{28,44},{32,4... | collective-permute-start | bytes 3145736 | tf_op jit(solution)/shard_map/cond/branch_3_fun/ppermute | solution.py:28
  102.2 50.7 %collective-permute-start.16 = (bf16[256,2048]{1,0:T(8,128)(2,1)}, bf16[256,2048]{1,0:T(8,128)(2,1)}, u32[]{:S(2)}, u32[]{:S(2)}) collective-permute-start(bf16[256,2048]{1,0:T(8,128)(2,1)} %get-tuple-element.88), channel_id=1, source_target_pairs={{0,16},{4,20},{8,24},{12,28},{16,32},{20,36},{24,40},{28,44},{32,4... | collective-permute-start | bytes 3145736 | tf_op jit(solution)/shard_map/cond/branch_3_fun/ppermute | solution.py:28
  126.1 49.2 %collective-permute-start.12 = (bf16[256,2048]{1,0:T(8,128)(2,1)S(1)}, bf16[256,2048]{1,0:T(8,128)(2,1)}, u32[]{:S(2)}, u32[]{:S(2)}) collective-permute-start(bf16[256,2048]{1,0:T(8,128)(2,1)S(1)} %collective-permute-done.11), channel_id=1, source_target_pairs={{0,16},{4,4},{8,8},{12,12},{16,32},{20,20},{24,24},{28,28},{32,48}... | collective-permute-start | bytes 3145736 | tf_op jit(solution)/shard_map/cond/branch_3_fun/ppermute | solution.py:295
  128.1 47.3 %collective-permute-start.15 = (bf16[256,2048]{1,0:T(8,128)(2,1)S(1)}, bf16[256,2048]{1,0:T(8,128)(2,1)}, u32[]{:S(2)}, u32[]{:S(2)}) collective-permute-start(bf16[256,2048]{1,0:T(8,128)(2,1)S(1)} %collective-permute-done.14), channel_id=1, source_target_pairs={{0,4},{4,8},{8,12},{12,0},{16,20},{20,24},{24,28},{28,16},{32,36},... | collective-permute-start | bytes 3145736 | tf_op jit(solution)/shard_map/cond/branch_3_fun/ppermute | solution.py:290
